TPU v7x, 32 devices: a whole 2x2x4 slice. The times are simulated.
32 devices in a mesh: groups: 2 (over x), shot: 16 (over z, y, core).
Axes of the slice: x: 2, y: 2, z: 4, core: 2. Of those that a mesh axis runs over, the one named last changes fastest.
Arguments:
- velocity: float32 [64, 4, 64, 128], P(('groups', 'shot')), parts along dimension 0, may hold values from 1.5 to 4
- tile_owner: int32 [32], replicated, may hold values from 0 to 15, as said below
- aperture: int32 [32, 16], P(('groups', 'shot')), parts along dimension 0, may hold values from 0 to 31, as said below
- source_at: int32 [32, 256], P(('groups', 'shot')), parts along dimension 0, may hold values from 0 to 524287
- source_amp: float32 [32, 256], P(('groups', 'shot')), parts along dimension 0, may hold values from -6 to 6
- receivers: int32 [32, 128], P(('groups', 'shot')), parts along dimension 0, may hold values from 0 to 524287
- wavelet: float32 [16], replicated, may hold values from -4 to 4
- observed: float32 [32, 16, 128], P(('groups', 'shot')), parts along dimension 0, may hold values from -6 to 6
Outputs:
- gradient: float32 [64, 4, 64, 128], P(('groups', 'shot')), parts along dimension 0
- misfit: float32 [32, 16, 128], P(('groups', 'shot')), parts along dimension 0
There are 2 independent parts, one for each index of `groups`. A program takes and returns all parts, laid end to end along the dimension named above; an argument that names none is the same for every part. Nothing has to cross between parts.
Inputs may be any that keep to these rules, and one draw needn't show every extreme that they name: tile_owner[t] depends only on t % 16, and distinct residues have distinct owners. `aperture`: each row holds 16 consecutive slab numbers in rising order.
All inputs are finite; a program needn't handle non-finite values.
Results may differ from a plain program's by a relative error of at most 0.0003.
Values sent between devices are 32-bit elements; how exact they have to be, the bound alone decides.
No kernel may reach another device: no remote copies, remote signals or barrier semaphores. Data moves between devices by JAX's collectives and lax.ppermute only.
A program may use at most 256 MiB of HBM per device.

v0:
```python
import jax
import jax.numpy as jnp
from jax import lax
from jax.sharding import PartitionSpec as P

COEF = (-205.0 / 72.0, 1.6, -0.2, 8.0 / 315.0, -1.0 / 560.0)
STEP_RATIO = 0.1


def laplace(field):
    padded = jnp.pad(field, 4)
    size_x, size_y, size_z = field.shape
    total = 3.0 * COEF[0] * field
    for k in range(1, 5):
        total = total + COEF[k] * (
            padded[4 + k : 4 + k + size_x, 4 : 4 + size_y, 4 : 4 + size_z]
            + padded[4 - k : 4 - k + size_x, 4 : 4 + size_y, 4 : 4 + size_z]
        )
        total = total + COEF[k] * (
            padded[4 : 4 + size_x, 4 + k : 4 + k + size_y, 4 : 4 + size_z]
            + padded[4 : 4 + size_x, 4 - k : 4 - k + size_y, 4 : 4 + size_z]
        )
        total = total + COEF[k] * (
            padded[4 : 4 + size_x, 4 : 4 + size_y, 4 + k : 4 + k + size_z]
            + padded[4 : 4 + size_x, 4 : 4 + size_y, 4 - k : 4 - k + size_z]
        )
    return total


def propagate(region, spots, amps, wavelet, listeners, recorded):
    shape = region.shape
    speed2 = (STEP_RATIO * region) ** 2
    zeros = jnp.zeros(shape, jnp.float32)

    def inject(field, where, values):
        return field.reshape(-1).at[where].add(values).reshape(shape)

    fields = [zeros]
    before = zeros
    current = zeros
    records = []
    for step in range(wavelet.shape[0]):
        nxt = 2.0 * current - before + speed2 * laplace(current)
        nxt = inject(nxt, spots, amps * wavelet[step])
        records.append(nxt.reshape(-1)[listeners])
        before, current = (current, nxt)
        fields.append(nxt)
    misfit = jnp.stack(records) - recorded
    after = zeros
    current = zeros
    image = zeros
    for step in range(wavelet.shape[0] - 1, -1, -1):
        nxt = 2.0 * current - after + speed2 * laplace(current)
        nxt = inject(nxt, listeners, misfit[step])
        after, current = (current, nxt)
        if step >= 1:
            image = image + nxt * (fields[step + 1] - 2.0 * fields[step] + fields[step - 1])
    return (misfit, 2.0 / region * image)


def shards(velocity, tile_owner, aperture, source_at, source_amp, receivers, wavelet, observed):
    devices = lax.axis_size("shot")
    per_dev = velocity.shape[0]
    cell_shape = velocity.shape[1:]
    slabs = aperture[0]
    owners = tile_owner[slabs]
    store_rows = owners * per_dev + slabs // devices
    empty = jnp.zeros((slabs.shape[0],) + cell_shape, jnp.float32)
    piece = lax.all_gather(velocity, "shot", axis=0, tiled=True)
    held = piece.shape[0]
    inside = (store_rows >= 0) & (store_rows < held)
    taken = piece[jnp.clip(store_rows, 0, held - 1)]
    pieces = jnp.where(inside[:, None, None, None], taken, empty)
    region = pieces.reshape((-1,) + cell_shape[1:])
    misfit, shot_grad = propagate(
        region, source_at[0], source_amp[0], wavelet, receivers[0], observed[0]
    )
    grad_slabs = shot_grad.reshape(pieces.shape)
    wanted_rows = jnp.arange(per_dev * lax.axis_size("shot"), dtype=jnp.int32)
    selector = (wanted_rows[:, None] == store_rows[None, :]).astype(jnp.float32)
    gradient = lax.psum_scatter(
        jnp.einsum("ra,axyz->rxyz", selector, grad_slabs, precision=lax.Precision.HIGHEST),
        "shot",
        scatter_dimension=0,
        tiled=True,
    )
    return (gradient, misfit[None])


def solution(mesh):
    in_specs = (
        P(("groups", "shot"), None, None, None),
        P(),
        P(("groups", "shot"), None),
        P(("groups", "shot"), None),
        P(("groups", "shot"), None),
        P(("groups", "shot"), None),
        P(),
        P(("groups", "shot"), None, None),
    )
    out_specs = (P(("groups", "shot"), None, None, None), P(("groups", "shot"), None, None))
    return jax.shard_map(shards, mesh=mesh, in_specs=in_specs, out_specs=out_specs, check_vma=False)
```

profile of v0, /device:TPU:0, one launch (start us, length us, event | category | flops | bytes accessed | tf_op | source)
XLA Modules:
  0.0 1231.2 jit_solution(10986702391235427648)
XLA Ops:
  14.8 10.7 broadcast_multiply_fusion
  25.5 38.1 %all-gather.2.cloned.1.call-done = f32[32,4,64,128]{3,2,1,0:T(8,128)} async-done(((f32[2,4,64,128]{3,2,1,0:T(8,128)}), f32[32,4,64,128]{3,2,1,0:T(8,128)}) %all-gather.2.cloned.1.call-update) | async-done | bytes 4194320 | tf_op jit(solution)/shard_map/all_gather | solution.py:69
  68.1 25.9 %fusion.1115 = f32[64,64,128]{2,1,0:T(8,128)} fusion(f32[64,64,128]{2,1,0:T(8,128)} %broadcast_in_dim.23, f32[16,4,64,128]{3,2,1,0:T(8,128)S(1)} %gather_fusion.1, pred[64]{0:T(512)(128)(4,1)S(1)} %broadcast_in_dim.21), kind=kLoop, calls=%fused_computation.1884 | loop fusion | flops 19398656 | bytes 6291520 | tf_op jit(solution)/shard_map/mul | solution.py:53
  97.1 4.8 scatter_fusion
  103.9 28.1 %fusion.15 = f32[64,64,128]{2,1,0:T(8,128)} fusion(f32[64,64,128]{2,1,0:T(8,128)} %bitcast.303, f32[16,4,64,128]{3,2,1,0:T(8,128)S(1)} %gather_fusion.1, pred[64]{0:T(512)(128)(4,1)S(1)} %broadcast_in_dim.21), kind=kLoop, calls=%fused_computation.784 | loop fusion | flops 22544384 | bytes 6291520 | tf_op jit(solution)/shard_map/add | solution.py:43
  132.0 5.0 scatter_fusion.1
  139.1 28.5 %fusion.53 = f32[64,64,128]{2,1,0:T(8,128)} fusion(f32[64,64,128]{2,1,0:T(8,128)} %bitcast.307, f32[64,64,128]{2,1,0:T(8,128)} %bitcast.304, f32[16,4,64,128]{3,2,1,0:T(8,128)S(1)} %gather_fusion.1, pred[64]{0:T(512)(128)(4,1)S(1)} %broadcast_in_dim.21), kind=kLoop, calls=%fused_computation.822 | loop fusion | flops 23068672 | bytes 8388672 | tf_op jit(solution)/shard_map/add | solution.py:43
  167.6 4.8 scatter_fusion.2
  174.6 30.9 %fusion.91 = f32[64,64,128]{2,1,0:T(8,128)} fusion(f32[64,64,128]{2,1,0:T(8,128)} %bitcast.311, f32[64,64,128]{2,1,0:T(8,128)} %bitcast.308, f32[16,4,64,128]{3,2,1,0:T(8,128)S(1)} %gather_fusion.1, pred[64]{0:T(512)(128)(4,1)S(1)} %broadcast_in_dim.21), kind=kLoop, calls=%fused_computation.860 | loop fusion | flops 23068672 | bytes 8388672 | tf_op jit(solution)/shard_map/add | solution.py:43
  205.5 4.9 scatter_fusion.3
  212.5 30.3 %fusion.129 = f32[64,64,128]{2,1,0:T(8,128)} fusion(f32[64,64,128]{2,1,0:T(8,128)} %bitcast.315, f32[64,64,128]{2,1,0:T(8,128)} %bitcast.312, f32[16,4,64,128]{3,2,1,0:T(8,128)S(1)} %gather_fusion.1, pred[64]{0:T(512)(128)(4,1)S(1)} %broadcast_in_dim.21), kind=kLoop, calls=%fused_computation.898 | loop fusion | flops 23068672 | bytes 8388672 | tf_op jit(solution)/shard_map/add | solution.py:43
  242.8 5.0 scatter_fusion.4
  249.9 28.4 %fusion.167 = f32[64,64,128]{2,1,0:T(8,128)} fusion(f32[64,64,128]{2,1,0:T(8,128)} %bitcast.319, f32[64,64,128]{2,1,0:T(8,128)} %bitcast.316, f32[16,4,64,128]{3,2,1,0:T(8,128)S(1)} %gather_fusion.1, pred[64]{0:T(512)(128)(4,1)S(1)} %broadcast_in_dim.21), kind=kLoop, calls=%fused_computation.936 | loop fusion | flops 23068672 | bytes 8388672 | tf_op jit(solution)/shard_map/add | solution.py:43
  278.3 4.9 scatter_fusion.5
  285.2 30.7 %fusion.205 = f32[64,64,128]{2,1,0:T(8,128)} fusion(f32[64,64,128]{2,1,0:T(8,128)} %bitcast.323, f32[64,64,128]{2,1,0:T(8,128)} %bitcast.320, f32[16,4,64,128]{3,2,1,0:T(8,128)S(1)} %gather_fusion.1, pred[64]{0:T(512)(128)(4,1)S(1)} %broadcast_in_dim.21), kind=kLoop, calls=%fused_computation.974 | loop fusion | flops 23068672 | bytes 8388672 | tf_op jit(solution)/shard_map/add | solution.py:43
  315.9 4.8 scatter_fusion.6
  322.9 30.2 %fusion.243 = f32[64,64,128]{2,1,0:T(8,128)} fusion(f32[64,64,128]{2,1,0:T(8,128)} %bitcast.327, f32[64,64,128]{2,1,0:T(8,128)} %bitcast.324, f32[16,4,64,128]{3,2,1,0:T(8,128)S(1)} %gather_fusion.1, pred[64]{0:T(512)(128)(4,1)S(1)} %broadcast_in_dim.21), kind=kLoop, calls=%fused_computation.1012 | loop fusion | flops 23068672 | bytes 8388672 | tf_op jit(solution)/shard_map/add | solution.py:43
  353.1 5.2 scatter_fusion.7
  360.5 29.1 %fusion.281 = f32[64,64,128]{2,1,0:T(8,128)} fusion(f32[64,64,128]{2,1,0:T(8,128)} %bitcast.331, f32[64,64,128]{2,1,0:T(8,128)} %bitcast.328, f32[16,4,64,128]{3,2,1,0:T(8,128)S(1)} %gather_fusion.1, pred[64]{0:T(512)(128)(4,1)S(1)} %broadcast_in_dim.21), kind=kLoop, calls=%fused_computation.1050 | loop fusion | flops 23068672 | bytes 8388672 | tf_op jit(solution)/shard_map/add | solution.py:43
  389.5 4.8 scatter_fusion.8
  396.4 29.2 %fusion.319 = f32[64,64,128]{2,1,0:T(8,128)} fusion(f32[64,64,128]{2,1,0:T(8,128)} %bitcast.335, f32[64,64,128]{2,1,0:T(8,128)} %bitcast.332, f32[16,4,64,128]{3,2,1,0:T(8,128)S(1)} %gather_fusion.1, pred[64]{0:T(512)(128)(4,1)S(1)} %broadcast_in_dim.21), kind=kLoop, calls=%fused_computation.1088 | loop fusion | flops 23068672 | bytes 8388672 | tf_op jit(solution)/shard_map/add | solution.py:43
  425.7 4.8 scatter_fusion.9
  432.6 28.5 %fusion.357 = f32[64,64,128]{2,1,0:T(8,128)} fusion(f32[64,64,128]{2,1,0:T(8,128)} %bitcast.339, f32[64,64,128]{2,1,0:T(8,128)} %bitcast.336, f32[16,4,64,128]{3,2,1,0:T(8,128)S(1)} %gather_fusion.1, pred[64]{0:T(512)(128)(4,1)S(1)} %broadcast_in_dim.21), kind=kLoop, calls=%fused_computation.1126 | loop fusion | flops 23068672 | bytes 8388672 | tf_op jit(solution)/shard_map/add | solution.py:43
  461.1 5.0 scatter_fusion.10
  468.2 29.5 %fusion.395 = f32[64,64,128]{2,1,0:T(8,128)} fusion(f32[64,64,128]{2,1,0:T(8,128)} %bitcast.343, f32[64,64,128]{2,1,0:T(8,128)} %bitcast.340, f32[16,4,64,128]{3,2,1,0:T(8,128)S(1)} %gather_fusion.1, pred[64]{0:T(512)(128)(4,1)S(1)} %broadcast_in_dim.21), kind=kLoop, calls=%fused_computation.1164 | loop fusion | flops 23068672 | bytes 8388672 | tf_op jit(solution)/shard_map/add | solution.py:43
  497.7 4.9 scatter_fusion.11
  504.7 30.6 %fusion.433 = f32[64,64,128]{2,1,0:T(8,128)} fusion(f32[64,64,128]{2,1,0:T(8,128)} %bitcast.347, f32[64,64,128]{2,1,0:T(8,128)} %bitcast.344, f32[16,4,64,128]{3,2,1,0:T(8,128)S(1)} %gather_fusion.1, pred[64]{0:T(512)(128)(4,1)S(1)} %broadcast_in_dim.21), kind=kLoop, calls=%fused_computation.1202 | loop fusion | flops 23068672 | bytes 8388672 | tf_op jit(solution)/shard_map/add | solution.py:43
  535.4 4.8 scatter_fusion.12
  542.3 29.1 %fusion.471 = f32[64,64,128]{2,1,0:T(8,128)} fusion(f32[64,64,128]{2,1,0:T(8,128)} %bitcast.351, f32[64,64,128]{2,1,0:T(8,128)} %bitcast.348, f32[16,4,64,128]{3,2,1,0:T(8,128)S(1)} %gather_fusion.1, pred[64]{0:T(512)(128)(4,1)S(1)} %broadcast_in_dim.21), kind=kLoop, calls=%fused_computation.1240 | loop fusion | flops 23068672 | bytes 8388672 | tf_op jit(solution)/shard_map/add | solution.py:43
  571.4 5.0 scatter_fusion.13
  578.6 29.8 %fusion.509 = f32[64,64,128]{2,1,0:T(8,128)} fusion(f32[64,64,128]{2,1,0:T(8,128)} %bitcast.355, f32[64,64,128]{2,1,0:T(8,128)} %bitcast.352, f32[16,4,64,128]{3,2,1,0:T(8,128)S(1)} %gather_fusion.1, pred[64]{0:T(512)(128)(4,1)S(1)} %broadcast_in_dim.21), kind=kLoop, calls=%fused_computation.1278 | loop fusion | flops 23068672 | bytes 8388672 | tf_op jit(solution)/shard_map/add | solution.py:43
  608.4 4.8 scatter_fusion.14
  615.3 29.0 %fusion.547 = f32[64,64,128]{2,1,0:T(8,128)} fusion(f32[64,64,128]{2,1,0:T(8,128)} %bitcast.410, f32[64,64,128]{2,1,0:T(8,128)} %bitcast.356, f32[16,4,64,128]{3,2,1,0:T(8,128)S(1)} %gather_fusion.1, pred[64]{0:T(512)(128)(4,1)S(1)} %broadcast_in_dim.21), kind=kLoop, calls=%fused_computation.1316 | loop fusion | flops 23068672 | bytes 8388672 | tf_op jit(solution)/shard_map/add | solution.py:43
  644.3 4.8 scatter_fusion.15
  651.4 4.2 scatter_fusion.16
  655.5 27.4 %fusion.585 = f32[64,64,128]{2,1,0:T(8,128)} fusion(f32[64,64,128]{2,1,0:T(8,128)} %bitcast.358, f32[16,4,64,128]{3,2,1,0:T(8,128)S(1)} %gather_fusion.1, pred[64]{0:T(512)(128)(4,1)S(1)} %broadcast_in_dim.21), kind=kLoop, calls=%fused_computation.1354 | loop fusion | flops 22544384 | bytes 6291520 | tf_op jit(solution)/shard_map/add | solution.py:53
  682.9 4.6 scatter_fusion.17
  687.5 29.6 %fusion.623 = f32[64,64,128]{2,1,0:T(8,128)} fusion(f32[64,64,128]{2,1,0:T(8,128)} %bitcast.362, f32[64,64,128]{2,1,0:T(8,128)} %bitcast.359, f32[16,4,64,128]{3,2,1,0:T(8,128)S(1)} %gather_fusion.1, pred[64]{0:T(512)(128)(4,1)S(1)} %broadcast_in_dim.21), kind=kLoop, calls=%fused_computation.1392 | loop fusion | flops 23068672 | bytes 8388672 | tf_op jit(solution)/shard_map/add | solution.py:53
  721.2 29.7 %fusion.661 = f32[64,64,128]{2,1,0:T(8,128)} fusion(f32[64,64,128]{2,1,0:T(8,128)} %bitcast.366, f32[64,64,128]{2,1,0:T(8,128)} %bitcast.363, f32[16,4,64,128]{3,2,1,0:T(8,128)S(1)} %gather_fusion.1, pred[64]{0:T(512)(128)(4,1)S(1)} %broadcast_in_dim.21), kind=kLoop, calls=%fused_computation.1430 | loop fusion | flops 23068672 | bytes 8388672 | tf_op jit(solution)/shard_map/add | solution.py:53
  750.9 4.1 scatter_fusion.19
  755.0 28.7 %fusion.699 = f32[64,64,128]{2,1,0:T(8,128)} fusion(f32[64,64,128]{2,1,0:T(8,128)} %bitcast.370, f32[64,64,128]{2,1,0:T(8,128)} %bitcast.367, f32[16,4,64,128]{3,2,1,0:T(8,128)S(1)} %gather_fusion.1, pred[64]{0:T(512)(128)(4,1)S(1)} %broadcast_in_dim.21), kind=kLoop, calls=%fused_computation.1468 | loop fusion | flops 23068672 | bytes 8388672 | tf_op jit(solution)/shard_map/add | solution.py:53
  783.6 4.2 scatter_fusion.20
  787.8 30.8 %fusion.737 = f32[64,64,128]{2,1,0:T(8,128)} fusion(f32[64,64,128]{2,1,0:T(8,128)} %bitcast.374, f32[64,64,128]{2,1,0:T(8,128)} %bitcast.371, f32[16,4,64,128]{3,2,1,0:T(8,128)S(1)} %gather_fusion.1, pred[64]{0:T(512)(128)(4,1)S(1)} %broadcast_in_dim.21), kind=kLoop, calls=%fused_computation.1506 | loop fusion | flops 23068672 | bytes 8388672 | tf_op jit(solution)/shard_map/add | solution.py:53
  818.6 4.2 scatter_fusion.21
  822.9 29.9 %fusion.775 = f32[64,64,128]{2,1,0:T(8,128)} fusion(f32[64,64,128]{2,1,0:T(8,128)} %bitcast.378, f32[64,64,128]{2,1,0:T(8,128)} %bitcast.375, f32[16,4,64,128]{3,2,1,0:T(8,128)S(1)} %gather_fusion.1, pred[64]{0:T(512)(128)(4,1)S(1)} %broadcast_in_dim.21), kind=kLoop, calls=%fused_computation.1544 | loop fusion | flops 23068672 | bytes 8388672 | tf_op jit(solution)/shard_map/add | solution.py:53
  852.7 4.2 scatter_fusion.22
  856.9 29.8 %fusion.813 = f32[64,64,128]{2,1,0:T(8,128)} fusion(f32[64,64,128]{2,1,0:T(8,128)} %bitcast.382, f32[64,64,128]{2,1,0:T(8,128)} %bitcast.379, f32[16,4,64,128]{3,2,1,0:T(8,128)S(1)} %gather_fusion.1, pred[64]{0:T(512)(128)(4,1)S(1)} %broadcast_in_dim.21), kind=kLoop, calls=%fused_computation.1582 | loop fusion | flops 23068672 | bytes 8388672 | tf_op jit(solution)/shard_map/add | solution.py:53
  886.7 4.1 scatter_fusion.23
  890.8 28.9 %fusion.851 = f32[64,64,128]{2,1,0:T(8,128)} fusion(f32[64,64,128]{2,1,0:T(8,128)} %bitcast.386, f32[64,64,128]{2,1,0:T(8,128)} %bitcast.383, f32[16,4,64,128]{3,2,1,0:T(8,128)S(1)} %gather_fusion.1, pred[64]{0:T(512)(128)(4,1)S(1)} %broadcast_in_dim.21), kind=kLoop, calls=%fused_computation.1620 | loop fusion | flops 23068672 | bytes 8388672 | tf_op jit(solution)/shard_map/add | solution.py:53
  919.7 4.1 scatter_fusion.24
  923.8 30.0 %fusion.889 = f32[64,64,128]{2,1,0:T(8,128)} fusion(f32[64,64,128]{2,1,0:T(8,128)} %bitcast.390, f32[64,64,128]{2,1,0:T(8,128)} %bitcast.387, f32[16,4,64,128]{3,2,1,0:T(8,128)S(1)} %gather_fusion.1, pred[64]{0:T(512)(128)(4,1)S(1)} %broadcast_in_dim.21), kind=kLoop, calls=%fused_computation.1658 | loop fusion | flops 23068672 | bytes 8388672 | tf_op jit(solution)/shard_map/add | solution.py:53
  953.8 4.4 scatter_fusion.25
  958.2 29.3 %fusion.927 = f32[64,64,128]{2,1,0:T(8,128)} fusion(f32[64,64,128]{2,1,0:T(8,128)} %bitcast.394, f32[64,64,128]{2,1,0:T(8,128)} %bitcast.391, f32[16,4,64,128]{3,2,1,0:T(8,128)S(1)} %gather_fusion.1, pred[64]{0:T(512)(128)(4,1)S(1)} %broadcast_in_dim.21), kind=kLoop, calls=%fused_computation.1696 | loop fusion | flops 23068672 | bytes 8388672 | tf_op jit(solution)/shard_map/add | solution.py:53
  991.6 28.9 %fusion.965 = f32[64,64,128]{2,1,0:T(8,128)} fusion(f32[64,64,128]{2,1,0:T(8,128)} %bitcast.398, f32[64,64,128]{2,1,0:T(8,128)} %bitcast.395, f32[16,4,64,128]{3,2,1,0:T(8,128)S(1)} %gather_fusion.1, pred[64]{0:T(512)(128)(4,1)S(1)} %broadcast_in_dim.21), kind=kLoop, calls=%fused_computation.1734 | loop fusion | flops 23068672 | bytes 8388672 | tf_op jit(solution)/shard_map/add | solution.py:53
  1020.5 4.1 scatter_fusion.27
  1024.6 28.2 %fusion.1003 = f32[64,64,128]{2,1,0:T(8,128)} fusion(f32[64,64,128]{2,1,0:T(8,128)} %bitcast.402, f32[64,64,128]{2,1,0:T(8,128)} %bitcast.399, f32[16,4,64,128]{3,2,1,0:T(8,128)S(1)} %gather_fusion.1, pred[64]{0:T(512)(128)(4,1)S(1)} %broadcast_in_dim.21), kind=kLoop, calls=%fused_computation.1772 | loop fusion | flops 23068672 | bytes 8388672 | tf_op jit(solution)/shard_map/add | solution.py:53
  1052.8 4.2 scatter_fusion.28
  1057.0 29.4 %fusion.1041 = f32[64,64,128]{2,1,0:T(8,128)} fusion(f32[64,64,128]{2,1,0:T(8,128)} %bitcast.406, f32[64,64,128]{2,1,0:T(8,128)} %bitcast.403, f32[16,4,64,128]{3,2,1,0:T(8,128)S(1)} %gather_fusion.1, pred[64]{0:T(512)(128)(4,1)S(1)} %broadcast_in_dim.21), kind=kLoop, calls=%fused_computation.1810 | loop fusion | flops 23068672 | bytes 8388672 | tf_op jit(solution)/shard_map/add | solution.py:53
  1086.5 4.3 scatter_fusion.29
  1090.8 28.6 %fusion.1079 = f32[64,64,128]{2,1,0:T(8,128)} fusion(f32[64,64,128]{2,1,0:T(8,128)} %bitcast.413, f32[64,64,128]{2,1,0:T(8,128)} %bitcast.407, f32[16,4,64,128]{3,2,1,0:T(8,128)S(1)} %gather_fusion.1, pred[64]{0:T(512)(128)(4,1)S(1)} %broadcast_in_dim.21), kind=kLoop, calls=%fused_computation.1848 | loop fusion | flops 23068672 | bytes 8388672 | tf_op jit(solution)/shard_map/add | solution.py:53
  1119.3 4.2 scatter_fusion.30
  1123.5 22.0 %add_multiply_fusion = f32[16,4,64,128]{3,2,1,0:T(8,128)S(1)} fusion(f32[16,4,64,128]{3,2,1,0:T(8,128)} %bitcast.418, f32[16,4,64,128]{3,2,1,0:T(8,128)} %bitcast.309, f32[16,4,64,128]{3,2,1,0:T(8,128)} %bitcast.305, f32[16,4,64,128]{3,2,1,0:T(8,128)} %bitcast.414, f32[16,4,64,128]{3,2,1,0:T(8,128)} %bitcast.313, f32[16,4,64,128]{3,2,1,0:T(8,128)} %bitcast.408, ...), kind=kLoop, calls=%fused_computation.1910 | loop fusion | flops 39845888 | bytes 69206032 | tf_op jit(solution)/shard_map/mul | solution.py:58
  1148.4 4.4 copy.15
  1153.5 70.4 %reduce-scatter.2.cloned.1.call-done = f32[2,4,64,128]{3,2,1,0:T(8,128)} async-done(((f32[32,4,64,128]{3,2,1,0:T(8,128)}), f32[2,4,64,128]{3,2,1,0:T(8,128)}) %reduce-scatter.2.cloned.1.call-update) | async-done | bytes 262160 | tf_op jit(solution)/shard_map/reduce_scatter | solution.py:81
  (52 shorter events, 60.6 us)
Async XLA Ops:
  7.2 1.5 copy-start
  7.2 56.5 %all-gather.2.cloned.1.call-start = ((), (), s32[]{:S(2)}) async-start(), calls=%async_computation.1 | async-start | bytes 4456448 | tf_op jit(solution)/shard_map/all_gather | solution.py:69
  7.9 1216.0 %reduce-scatter.2.cloned.1.call-start = ((), (), s32[]{:S(2)}) async-start(), calls=%async_computation.2 | async-start | bytes 4456448 | tf_op jit(solution)/shard_map/reduce_scatter | solution.py:81
  11.5 90.4 %copy-start.2 = (s32[1024]{0:T(1024)}, s32[1024]{0:T(1024)S(1)}, u32[]{:S(2)}) copy-start(s32[1024]{0:T(1024)S(1)} %pad_clamp_fusion) | copy-start | bytes 12292
  644.3 7.0 copy-start.3
  1152.8 71.1 %copy-start.1 = (s32[32]{0:T(128)S(1)}, s32[32]{0:T(128)}, u32[]{:S(2)}) copy-start(s32[32]{0:T(128)} %param.9) | copy-start | bytes 388
Sparse Core Ops, SparseCore 0:
  10.2 53.4 all-gather.1
  1152.9 70.8 reduce-scatter.1
where the time goes:
time: 1240 us; the launch traced here: 1230 us
  other arithmetic  1060 us (85%)
  waiting for transfers between devices  109 us (9%)
  local copies, waits for them, and re-layouts  48.4 us (4%)
  between operations  14.9 us (1%)
    add x15, other arithmetic, propagate(): nxt = 2.0 * current - before + speed2 * laplace(current)  442 us
    add x14, other arithmetic, propagate(): nxt = 2.0 * current - after + speed2 * laplace(current)  409 us
    scatter-add x31, other arithmetic, inject(): return field.reshape(-1).at[where].add(values).reshape(shape)  141 us
    reduce_scatter x1, waiting for transfers between devices, shards(): lax.psum_scatter(jnp.einsum('ra,axyz->rxyz', selector, grad_slabs, precis...  70.4 us
    all_gather x1, waiting for transfers between devices, shards(): piece = lax.all_gather(velocity, 'shot', axis=0, tiled=True)  38.1 us
    gather x16, local copies, waits for them, and re-layouts, propagate(): records.append(nxt.reshape(-1)[listeners])  33.6 us
    mul x1, other arithmetic, propagate(): nxt = 2.0 * current - after + speed2 * laplace(current)  25.9 us
  transfers between devices with their start and end apart: 2, of which 2 were waited for; matrix products, arithmetic and copies ran while one was open for 1% of the time, Pallas kernels for 0%

commit v1 on v0

v1 whole, which is shorter than its diff:
```python
import jax
import jax.numpy as jnp
import numpy as np
from jax import lax
from jax.experimental import pallas as pl
from jax.experimental.pallas import tpu as pltpu
from jax.sharding import PartitionSpec as P

STEP_RATIO = 0.1
TAPS = (63.0, -7.875, 1.0, -0.0703125)
CENTER_Z = -336.0
CENTER_Y = -0.328125
SCALE = 128.0 / 5040.0
REACH = 4
LANES = 128
GROUP = 4


def band(size, center):
    out = np.zeros((size, size), np.float32)
    np.fill_diagonal(out, center)
    for k, tap in enumerate(TAPS, 1):
        at = np.arange(size - k)
        out[at, at + k] = tap
        out[at + k, at] = tap
    return out


def kernel(
    rows_ref, slot_ref, rec_ref, wav_ref,
    vel_ref, src_hbm, pick_ref, same_ref, obs_ref, mat_y_ref, mat_z_ref,
    grad_ref, mis_ref,
    hist, field, halves, speed, region, dense, rate, rec_rows, moved, in_sem, src_sem, out_sem,
):
    nstep, cells, _ = hist.shape
    nrec = pick_ref.shape[0]
    ny = mat_y_ref.shape[0] // 2
    slab = vel_ref.shape[1]
    edge = REACH * ny
    block = GROUP * ny
    groups = cells // block
    held = slot_ref.shape[0]

    def fetch(j):
        return pltpu.make_async_copy(
            vel_ref.at[rows_ref[j]], region.at[pl.ds(j * slab, slab), :], in_sem.at[j]
        )

    def blank(r):
        return pltpu.make_async_copy(field.at[0, pl.ds(0, slab), :], grad_ref.at[r], out_sem.at[r])

    def give(r):
        at = pl.multiple_of(jnp.maximum(slot_ref[r], 0) * slab, slab)
        return pltpu.make_async_copy(dense.at[pl.ds(at, slab), :], grad_ref.at[r], out_sem.at[r])

    source = pltpu.make_async_copy(src_hbm, dense, src_sem)
    source.start()
    for j in range(rows_ref.shape[0]):
        fetch(j).start()

    zeros = jnp.zeros((edge, LANES), jnp.float32)
    for b in range(2):
        field[b, 0:edge, :] = zeros
        field[b, edge + cells : edge + cells + edge, :] = zeros

    for r in range(held):
        @pl.when(slot_ref[r] < 0)
        def _():
            blank(r).start()

    def keep(at, value):
        high = value.astype(jnp.bfloat16)
        halves[pl.ds(at, 16), 0:LANES] = high
        halves[pl.ds(at, 16), LANES : 2 * LANES] = (value - high.astype(jnp.float32)).astype(jnp.bfloat16)

    def listen(n, b):
        def body(r, _):
            rec_rows[n, pl.ds(r, 1), :] = field[b, pl.ds(edge + rec_ref[r], 1), :]
            return 0

        lax.fori_loop(0, nrec, body, 0, unroll=16)

    def sweep(cur, update):
        def body(g, _):
            base = pl.multiple_of(g * block, block)
            both = halves[pl.ds(base, block), :]
            along_z = jnp.dot(both, mat_z_ref[...], preferred_element_type=jnp.float32)
            plane = [both[i * ny : (i + 1) * ny] for i in range(GROUP)]
            cols = []
            for i in range(0, GROUP, 2):
                cols.append(
                    jnp.concatenate(
                        [plane[i][:, :LANES], plane[i][:, LANES:], plane[i + 1][:, :LANES], plane[i + 1][:, LANES:]],
                        axis=0,
                    )
                )
            along_y = jnp.dot(
                mat_y_ref[...], jnp.concatenate(cols, axis=1), preferred_element_type=jnp.float32
            )
            for j in range(0, ny, 16):
                near = [
                    field[cur, pl.ds(base + d * ny + j, 16), :] for d in range(GROUP + 2 * REACH)
                ]
                for i in range(GROUP):
                    lap = near[i + 4 - 3] + near[i + 4 + 3]
                    lap = lap + TAPS[0] * (near[i + 4 - 1] + near[i + 4 + 1])
                    lap = lap + TAPS[1] * (near[i + 4 - 2] + near[i + 4 + 2])
                    lap = lap + TAPS[3] * (near[i + 4 - 4] + near[i + 4 + 4])
                    lap = lap + along_z[i * ny + j : i * ny + j + 16]
                    at_y = (i % 2) * ny + j
                    lap = lap + along_y[at_y : at_y + 16, (i // 2) * LANES : (i // 2 + 1) * LANES]
                    at = pl.multiple_of(base + i * ny + j, 16)
                    update(at, near[i + 4], lap)
            return 0

        lax.fori_loop(0, groups, body, 0)

    def rows16(fn):
        def body(g, _):
            fn(pl.multiple_of(g * 16, 16))
            return 0

        lax.fori_loop(0, cells // 16, body, 0, unroll=4)

    source.wait()

    def first(at):
        value = wav_ref[0] * dense[pl.ds(at, 16), :]
        hist[0, pl.ds(at, 16), :] = value
        field[0, pl.ds(edge + at, 16), :] = value
        keep(at, value)

    rows16(first)
    listen(0, 0)

    for j in range(rows_ref.shape[0]):
        fetch(j).wait()

    def squared(at):
        scaled = STEP_RATIO * region[pl.ds(at, 16), :]
        speed[pl.ds(at, 16), :] = (scaled * scaled) * SCALE

    rows16(squared)

    def forward(n, _):
        cur = (n - 1) & 1
        new = n & 1
        strength = wav_ref[n]

        def update(at, here, lap):
            here_rate = hist[n - 1, pl.ds(at, 16), :] + (
                speed[pl.ds(at, 16), :] * lap + strength * dense[pl.ds(at, 16), :]
            )
            value = here + here_rate
            hist[n, pl.ds(at, 16), :] = here_rate
            field[new, pl.ds(edge + at, 16), :] = value
            keep(at, value)

        sweep(cur, update)
        listen(n, new)
        return 0

    lax.fori_loop(1, nstep, forward, 0)

    step_lane = lax.broadcasted_iota(jnp.int32, (nrec, nstep), 1)

    def compare(n, total):
        picked = jnp.sum(rec_rows[n] * pick_ref[...], axis=1, keepdims=True)
        total = jnp.where(step_lane == n, picked, total)
        seen = jnp.sum(jnp.where(step_lane == n, obs_ref[...], 0.0), axis=1, keepdims=True)
        rec_rows[n] = jnp.dot(
            same_ref[...], pick_ref[...] * (picked - seen),
            preferred_element_type=jnp.float32, precision=lax.Precision.HIGHEST,
        )
        return total

    records = lax.fori_loop(0, nstep, compare, jnp.zeros((nrec, nstep), jnp.float32))
    mis_ref[...] = records - obs_ref[...]

    def inject(n):
        def take(r, _):
            moved[pl.ds(r, 1), :] = rate[pl.ds(rec_ref[r], 1), :]
            return 0

        lax.fori_loop(0, nrec, take, 0, unroll=16)
        moved[...] = moved[...] + rec_rows[n]

        def put(r, _):
            rate[pl.ds(rec_ref[r], 1), :] = moved[pl.ds(r, 1), :]
            return 0

        lax.fori_loop(0, nrec, put, 0, unroll=16)

    def clear(at):
        rate[pl.ds(at, 16), :] = jnp.zeros((16, LANES), jnp.float32)

    rows16(clear)
    inject(nstep - 1)

    def last(at):
        value = rate[pl.ds(at, 16), :]
        field[(nstep - 1) & 1, pl.ds(edge + at, 16), :] = value
        dense[pl.ds(at, 16), :] = hist[nstep - 1, pl.ds(at, 16), :] * value
        keep(at, value)

    rows16(last)

    def backward(k, _):
        n = nstep - 1 - k
        inject(n - 1)

        def update(at, here, lap):
            here_rate = rate[pl.ds(at, 16), :] + speed[pl.ds(at, 16), :] * lap
            value = here + here_rate
            rate[pl.ds(at, 16), :] = here_rate
            field[(n - 1) & 1, pl.ds(edge + at, 16), :] = value
            dense[pl.ds(at, 16), :] = dense[pl.ds(at, 16), :] + hist[n - 1, pl.ds(at, 16), :] * here_rate
            keep(at, value)

        sweep(n & 1, update)
        return 0

    lax.fori_loop(0, nstep - 2, backward, 0)

    def finish(at):
        image = dense[pl.ds(at, 16), :] - hist[0, pl.ds(at, 16), :] * field[1, pl.ds(edge + at, 16), :]
        dense[pl.ds(at, 16), :] = (2.0 / region[pl.ds(at, 16), :]) * image

    rows16(finish)

    for r in range(held):
        @pl.when(slot_ref[r] >= 0)
        def _():
            give(r).start()

    for r in range(held):
        blank(r).wait()


def shot(store_rows, slots, rec_at, wavelet, pieces, sources, picks, same, observed):
    held, slab = pieces.shape[0], pieces.shape[1] * pieces.shape[2]
    ny, nz = pieces.shape[2:]
    aper = store_rows.shape[0]
    cells = aper * slab
    nstep, nrec = wavelet.shape[0], rec_at.shape[0]
    in_y = band(ny, CENTER_Y)
    none = np.zeros_like(in_y)
    mat_y = np.block([[in_y, in_y, none, none], [none, none, in_y, in_y]])
    in_z = band(nz, CENTER_Z)
    mat_z = np.concatenate([in_z, in_z], axis=0)
    smem = pl.BlockSpec(memory_space=pltpu.SMEM)
    vmem = pl.BlockSpec(memory_space=pltpu.VMEM)
    hbm = pl.BlockSpec(memory_space=pl.ANY)
    f32 = jnp.float32
    edge = REACH * ny
    grad, misfit = pl.pallas_call(
        kernel,
        out_shape=(
            jax.ShapeDtypeStruct((held, slab, nz), f32),
            jax.ShapeDtypeStruct((nrec, nstep), f32),
        ),
        in_specs=[smem] * 4 + [hbm] * 2 + [vmem] * 5,
        out_specs=(hbm, vmem),
        scratch_shapes=[
            pltpu.VMEM((nstep, cells, nz), f32),
            pltpu.VMEM((2, cells + 2 * edge, nz), f32),
            pltpu.VMEM((cells, 2 * nz), jnp.bfloat16),
            pltpu.VMEM((cells, nz), f32),
            pltpu.VMEM((cells, nz), f32),
            pltpu.VMEM((cells, nz), f32),
            pltpu.VMEM((cells, nz), f32),
            pltpu.VMEM((nstep, nrec, nz), f32),
            pltpu.VMEM((nrec, nz), f32),
            pltpu.SemaphoreType.DMA((aper,)),
            pltpu.SemaphoreType.DMA,
            pltpu.SemaphoreType.DMA((held,)),
        ],
        compiler_params=pltpu.CompilerParams(vmem_limit_bytes=60 * 1024 * 1024),
        name="shot_gradient",
    )(
        store_rows, slots, rec_at, wavelet,
        pieces.reshape(held, slab, nz), sources, picks, same, observed,
        jnp.asarray(mat_y, jnp.bfloat16), jnp.asarray(mat_z, jnp.bfloat16),
    )
    return grad.reshape(pieces.shape), misfit


def shards(velocity, tile_owner, aperture, source_at, source_amp, receivers, wavelet, observed):
    devices = lax.axis_size("shot")
    per_dev = velocity.shape[0]
    slabs = aperture[0]
    store_rows = tile_owner[slabs] * per_dev + slabs // devices
    pieces = lax.all_gather(velocity, "shot", axis=0, tiled=True)
    held = pieces.shape[0]
    nz = velocity.shape[3]
    hit = jnp.arange(held, dtype=jnp.int32)[:, None] == store_rows[None, :]
    slots = jnp.max(jnp.where(hit, jnp.arange(slabs.shape[0], dtype=jnp.int32)[None, :], -1), axis=1)
    cells = slabs.shape[0] * velocity.shape[1] * velocity.shape[2]
    sources = jnp.zeros((cells * nz,), jnp.float32).at[source_at[0]].add(source_amp[0]).reshape(cells, nz)
    rec_at = receivers[0] // nz
    lane = receivers[0] % nz
    picks = (lane[:, None] == jnp.arange(nz, dtype=jnp.int32)[None, :]).astype(jnp.float32)
    same = (rec_at[:, None] == rec_at[None, :]).astype(jnp.float32)
    grad, misfit = shot(store_rows, slots, rec_at, wavelet, pieces, sources, picks, same, observed[0].T)
    gradient = lax.psum_scatter(grad, "shot", scatter_dimension=0, tiled=True)
    return (gradient, misfit.T[None])


def solution(mesh):
    in_specs = (
        P(("groups", "shot"), None, None, None),
        P(),
        P(("groups", "shot"), None),
        P(("groups", "shot"), None),
        P(("groups", "shot"), None),
        P(("groups", "shot"), None),
        P(),
        P(("groups", "shot"), None, None),
    )
    out_specs = (P(("groups", "shot"), None, None, None), P(("groups", "shot"), None, None))
    return jax.shard_map(shards, mesh=mesh, in_specs=in_specs, out_specs=out_specs, check_vma=False)
```

time: 1240 us -> 305 us (0.25)
  other arithmetic: 1060 us -> 6.82 us
  Pallas kernels: 0 us -> 163 us
  local copies, waits for them, and re-layouts: 48.4 us -> 3.57 us
    add x29 -> x1, other arithmetic: 851 us -> 0.52 us  [shards(): store_rows = tile_owner[slabs] * per_dev + slabs // devices]
    pallas_call x0 -> x1, Pallas kernels: none -> 163 us  [shot(): pl.pallas_call(kernel, out_shape=(jax.ShapeDtypeStruct((held, slab, nz),...]
    scatter-add x31 -> x1, other arithmetic: 141 us -> 3.55 us  [shards(): jnp.zeros((cells * nz,), jnp.float32).at[source_at[0]].add(source_amp[0])]
    mul x3 -> x0, other arithmetic: 58.6 us -> none  [the longest x1 25.9 us: propagate(): nxt = 2.0 * current - after + speed2 * laplace(current)]
    gather x18 -> x1, local copies, waits for them, and re-layouts: 37.1 us -> 0.66 us  [shards(): store_rows = tile_owner[slabs] * per_dev + slabs // devices]
  transfers between devices with their start and end apart: 2 -> 2, of which waited for: 2 -> 2; matrix products, arithmetic and copies ran while one was open for 1% -> 3% of each run, Pallas kernels for 0% -> 0%
where the time goes in v1:
time: 305 us; the launch traced here: 304 us
  Pallas kernels  163 us (53%)
  waiting for transfers between devices  117 us (38%)
  between operations  14.1 us (5%)
  other arithmetic  6.82 us (2%)
  local copies, waits for them, and re-layouts  3.57 us (1%)
    pallas_call x1, Pallas kernels, shot(): pl.pallas_call(kernel, out_shape=(jax.ShapeDtypeStruct((held, slab, nz),...  163 us
    reduce_scatter x1, waiting for transfers between devices, shards(): gradient = lax.psum_scatter(grad, 'shot', scatter_dimension=0, tiled=True)  69.6 us
    all_gather x1, waiting for transfers between devices, shards(): pieces = lax.all_gather(velocity, 'shot', axis=0, tiled=True)  46.6 us
  transfers between devices with their start and end apart: 2, of which 2 were waited for; matrix products, arithmetic and copies ran while one was open for 3% of the time, Pallas kernels for 0%

profile of v1, /device:TPU:0, one launch (start us, length us, event | category | flops | bytes accessed | tf_op | source)
XLA Modules:
  0.0 304.1 jit_solution(5376916983838672077)
XLA Ops:
  7.2 0.0 copy-start
  7.2 0.0 copy-start.4
  7.2 0.0 copy-start.3
  7.2 0.0 all-gather.2.cloned.1.call-start
  7.2 0.7 all-gather.2.cloned.1.call-update
  7.9 0.0 reduce-scatter.2.cloned.1.call-start
  8.0 1.4 copy.18
  9.4 0.7 fusion.3
  10.1 0.0 copy-done
  10.1 0.7 gather_fusion
  10.7 0.7 compare_select_fusion
  11.4 3.5 %scatter_custom_fusion = f32[524288]{0:T(1024)} fusion(s32[256]{0:T(256)S(1)} %bitcast.55, f32[256]{0:T(256)} %bitcast.56, f32[]{:T(128)} %constant.55.clone.1), kind=kCustom, calls=%fused_computation.2 | custom fusion | flops 256 | bytes 2097664 | tf_op jit(solution)/shard_map/scatter-add | solution.py:299
  15.0 0.0 copy-done.4
  15.0 0.6 select_reduce_fusion.slot_ref
  15.6 0.0 copy-done.3
  15.6 0.0 copy-start.2
  15.6 0.5 fusion.6.rows_ref
  16.2 0.7 fusion.2
  16.9 46.6 %all-gather.2.cloned.1.call-done = f32[32,4,64,128]{3,2,1,0:T(8,128)} async-done(((f32[2,4,64,128]{3,2,1,0:T(8,128)}), f32[32,4,64,128]{3,2,1,0:T(8,128)}) %all-gather.2.cloned.1.call-update) | async-done | bytes 4194320 | tf_op jit(solution)/shard_map/all_gather | solution.py:293
  63.5 0.0 copy-done.2
  63.5 162.6 %shot_gradient.1 = (f32[32,256,128]{2,1,0:T(8,128)}, f32[128,16]{1,0:T(8,128)}) custom-call(s32[16]{0:T(128)} %fusion.6.rows_ref, s32[32]{0:T(128)} %select_reduce_fusion.slot_ref, s32[128]{0:T(128)} %copy-done.2, f32[16]{0:T(128)} %wav_ref.1, f32[32,256,128]{2,1,0:T(8,128)} %bitcast.51, f32[4096,128]{1,0:T(8,128)} %bitcast.50, ...), custom_call_target="tpu_custom_call" | custom-call | tf_op jit(solution)/shard_map/shot_gradient/pallas_call | solution.py:256
  226.1 0.0 copy-start.1
  226.1 0.0 reduce-scatter.2.cloned.1.call-update
  226.2 0.8 copy-done.1
  227.0 0.7 copy.19
  227.6 69.6 %reduce-scatter.2.cloned.1.call-done = f32[2,4,64,128]{3,2,1,0:T(8,128)} async-done(((f32[32,4,64,128]{3,2,1,0:T(8,128)}), f32[2,4,64,128]{3,2,1,0:T(8,128)}) %reduce-scatter.2.cloned.1.call-update) | async-done | bytes 262160 | tf_op jit(solution)/shard_map/reduce_scatter | solution.py:305
  (4 shorter events, 0.0 us)
Async XLA Ops:
  7.2 2.9 copy-start
  7.2 7.8 %copy-start.4 = (s32[1,16]{1,0:T(1,128)S(1)}, s32[1,16]{1,0:T(1,128)}, u32[]{:S(2)}) copy-start(s32[1,16]{1,0:T(1,128)} %param.12) | copy-start | bytes 196
  7.2 8.4 %copy-start.3 = (s32[1,128]{1,0:T(1,128)S(1)}, s32[1,128]{1,0:T(1,128)}, u32[]{:S(2)}) copy-start(s32[1,128]{1,0:T(1,128)} %param.15) | copy-start | bytes 1540
  7.2 56.3 %all-gather.2.cloned.1.call-start = ((), (), s32[]{:S(2)}) async-start(), calls=%async_computation.1 | async-start | bytes 4456448 | tf_op jit(solution)/shard_map/all_gather | solution.py:293
  7.9 289.3 %reduce-scatter.2.cloned.1.call-start = ((), (), s32[]{:S(2)}) async-start(), calls=%async_computation.2 | async-start | bytes 4456448 | tf_op jit(solution)/shard_map/reduce_scatter | solution.py:305
  15.6 47.9 %copy-start.2 = (s32[128]{0:T(128)}, s32[128]{0:T(128)S(1)}, u32[]{:S(2)}) copy-start(s32[128]{0:T(128)S(1)} %get-tuple-element.15.rec_ref) | copy-start | bytes 1540
  226.1 0.8 copy-start.1
Sparse Core Ops, SparseCore 0:
  10.2 53.2 all-gather.1
  226.3 70.9 reduce-scatter.1

commit v2 on v1

v2 whole, which is shorter than its diff:
```python
import functools

import jax
import jax.numpy as jnp
import numpy as np
from jax import lax
from jax.experimental import pallas as pl
from jax.experimental.pallas import tpu as pltpu
from jax.sharding import PartitionSpec as P

STEP_RATIO = 0.1
TAPS = (63.0, -7.875, 1.0, -0.0703125)
CENTER_Z = -336.0
CENTER_Y = -0.328125
SCALE = 128.0 / 5040.0
REACH = 4
LANES = 128
GROUP = 8


def band(size, center):
    out = np.zeros((size, size), np.float32)
    np.fill_diagonal(out, center)
    for k, tap in enumerate(TAPS, 1):
        at = np.arange(size - k)
        out[at, at + k] = tap
        out[at + k, at] = tap
    return out


def kernel(
    sources, targets, take_ref, give_ref, rec_ref, wav_ref, src_hbm, pick_ref, same_ref, obs_ref, mat_y_ref, mat_z_ref,
    *refs,
):
    vel_refs, refs = refs[:sources], refs[sources:]
    grad_refs, refs = refs[:targets], refs[targets:]
    (
        mis_ref, hist_a, hist_b, field_a, field_b, halves_a, halves_b, taps_a, taps_b,
        speed, region, dense, rate, rec_rows, moved, in_sem, src_sem, out_sem,
    ) = refs
    nstep = wav_ref.shape[0]
    cells = speed.shape[0]
    nrec = pick_ref.shape[0]
    ny = mat_y_ref.shape[0] // 2
    per, slab = vel_refs[0].shape[:2]
    out_per = grad_refs[0].shape[0]
    aper = cells // slab
    edge = REACH * ny
    block = GROUP * ny
    groups = cells // block
    held = give_ref.shape[0]

    def fetch(i, j):
        at = pl.multiple_of(j * slab, slab)
        return pltpu.make_async_copy(
            vel_refs[i // per].at[i % per], region.at[pl.ds(at, slab), :], in_sem.at[j]
        )

    def blank(r):
        return pltpu.make_async_copy(
            field_a.at[pl.ds(0, slab), :], grad_refs[r // out_per].at[r % out_per], out_sem.at[r]
        )

    def give(r):
        at = pl.multiple_of(give_ref[r] * slab, slab)
        return pltpu.make_async_copy(
            dense.at[pl.ds(at, slab), :], grad_refs[r // out_per].at[r % out_per], out_sem.at[r]
        )

    source = pltpu.make_async_copy(src_hbm, dense, src_sem)
    source.start()
    for i in range(sources * per):
        @pl.when(take_ref[i] >= 0)
        def _():
            fetch(i, take_ref[i]).start()

    zeros = jnp.zeros((edge, LANES), jnp.float32)
    for field in (field_a, field_b):
        field[0:edge, :] = zeros
        field[edge + cells : edge + cells + edge, :] = zeros

    for r in range(held):
        @pl.when(give_ref[r] < 0)
        def _():
            blank(r).start()

    fields = (field_a, field_b)
    hist = (hist_a, hist_b)
    halves = (halves_a, halves_b)

    def keep(to, at, value):
        high = value.astype(jnp.bfloat16)
        halves[to][pl.ds(at, 16), 0:LANES] = high
        halves[to][pl.ds(at, 16), LANES : 2 * LANES] = (value - high.astype(jnp.float32)).astype(jnp.bfloat16)

    def listen(n, to):
        def body(r, _):
            rec_rows[n, pl.ds(r, 1), :] = fields[to][pl.ds(edge + rec_ref[r], 1), :]
            return 0

        lax.fori_loop(0, nrec, body, 0, unroll=16)

    def multiply(base, of, taps):
        both = halves[of][pl.ds(base, block), :]
        along_z = jnp.dot(both, mat_z_ref[...], preferred_element_type=jnp.float32)
        plane = [both[i * ny : (i + 1) * ny] for i in range(GROUP)]
        cols = []
        for i in range(0, GROUP, 2):
            cols.append(
                jnp.concatenate(
                    [plane[i][:, :LANES], plane[i][:, LANES:], plane[i + 1][:, :LANES], plane[i + 1][:, LANES:]],
                    axis=0,
                )
            )
        along_y = jnp.dot(mat_y_ref[...], jnp.concatenate(cols, axis=1), preferred_element_type=jnp.float32)
        for i in range(GROUP):
            taps[i * ny : (i + 1) * ny, :] = (
                along_z[i * ny : (i + 1) * ny]
                + along_y[(i % 2) * ny : (i % 2 + 1) * ny, (i // 2) * LANES : (i // 2 + 1) * LANES]
            )

    def combine(base, of, taps, update):
        for j in range(0, ny, 16):
            near = [fields[of][pl.ds(base + d * ny + j, 16), :] for d in range(GROUP + 2 * REACH)]
            for i in range(GROUP):
                lap = near[i + 4 - 3] + near[i + 4 + 3]
                lap = lap + TAPS[0] * (near[i + 4 - 1] + near[i + 4 + 1])
                lap = lap + TAPS[1] * (near[i + 4 - 2] + near[i + 4 + 2])
                lap = lap + TAPS[3] * (near[i + 4 - 4] + near[i + 4 + 4])
                lap = lap + taps[i * ny + j : i * ny + j + 16, :]
                at = base + i * ny + j
                update(at if isinstance(at, int) else pl.multiple_of(at, 16), near[i + 4], lap)

    def sweep(of, update):
        def body(g, _):
            base = pl.multiple_of(g * (2 * block), 2 * block)
            multiply(base + block, of, taps_b)
            combine(base, of, taps_a, update)
            multiply(base + 2 * block, of, taps_a)
            combine(base + block, of, taps_b, update)
            return 0

        lax.fori_loop(0, groups // 2 - 1, body, 0)
        base = (groups - 2) * block
        multiply(base + block, of, taps_b)
        combine(base, of, taps_a, update)
        multiply(0, 1 - of, taps_a)
        combine(base + block, of, taps_b, update)

    def rows16(fn):
        def body(g, _):
            fn(pl.multiple_of(g * 16, 16))
            return 0

        lax.fori_loop(0, cells // 16, body, 0, unroll=4)

    source.wait()

    def first(at):
        value = wav_ref[0] * dense[pl.ds(at, 16), :]
        hist_a[0, pl.ds(at, 16), :] = value
        field_a[pl.ds(edge + at, 16), :] = value
        keep(0, at, value)

    rows16(first)
    multiply(0, 0, taps_a)
    listen(0, 0)

    for j in range(aper):
        fetch(0, j).wait()

    def squared(at):
        scaled = STEP_RATIO * region[pl.ds(at, 16), :]
        speed[pl.ds(at, 16), :] = (scaled * scaled) * SCALE

    rows16(squared)

    def forward(n, of):
        strength = wav_ref[n]

        def update(at, here, lap):
            here_rate = hist[of][(n - 1) // 2, pl.ds(at, 16), :] + (
                speed[pl.ds(at, 16), :] * lap + strength * dense[pl.ds(at, 16), :]
            )
            value = here + here_rate
            hist[1 - of][n // 2, pl.ds(at, 16), :] = here_rate
            fields[1 - of][pl.ds(edge + at, 16), :] = value
            keep(1 - of, at, value)

        sweep(of, update)
        listen(n, 1 - of)

    def forward_pair(k, _):
        forward(2 * k + 1, 0)
        forward(2 * k + 2, 1)
        return 0

    lax.fori_loop(0, (nstep - 1) // 2, forward_pair, 0)
    if nstep % 2 == 0:
        forward(nstep - 1, 0)

    step_lane = lax.broadcasted_iota(jnp.int32, (nrec, nstep), 1)

    def compare(n, total):
        picked = jnp.sum(rec_rows[n] * pick_ref[...], axis=1, keepdims=True)
        total = jnp.where(step_lane == n, picked, total)
        seen = jnp.sum(jnp.where(step_lane == n, obs_ref[...], 0.0), axis=1, keepdims=True)
        rec_rows[n] = jnp.dot(
            same_ref[...], pick_ref[...] * (picked - seen),
            preferred_element_type=jnp.float32, precision=lax.Precision.HIGHEST,
        )
        return total

    records = lax.fori_loop(0, nstep, compare, jnp.zeros((nrec, nstep), jnp.float32))
    mis_ref[...] = records - obs_ref[...]

    def inject(n):
        def take(r, _):
            moved[pl.ds(r, 1), :] = rate[pl.ds(rec_ref[r], 1), :]
            return 0

        lax.fori_loop(0, nrec, take, 0, unroll=16)
        moved[...] = moved[...] + rec_rows[n]

        def put(r, _):
            rate[pl.ds(rec_ref[r], 1), :] = moved[pl.ds(r, 1), :]
            return 0

        lax.fori_loop(0, nrec, put, 0, unroll=16)

    def clear(at):
        rate[pl.ds(at, 16), :] = jnp.zeros((16, LANES), jnp.float32)

    rows16(clear)
    inject(nstep - 1)

    def last(at):
        value = rate[pl.ds(at, 16), :]
        field_a[pl.ds(edge + at, 16), :] = value
        dense[pl.ds(at, 16), :] = hist[(nstep - 1) % 2][(nstep - 1) // 2, pl.ds(at, 16), :] * value
        keep(0, at, value)

    rows16(last)
    multiply(0, 0, taps_a)

    def backward(n, of):
        inject(n - 1)

        def update(at, here, lap):
            here_rate = rate[pl.ds(at, 16), :] + speed[pl.ds(at, 16), :] * lap
            value = here + here_rate
            rate[pl.ds(at, 16), :] = here_rate
            fields[1 - of][pl.ds(edge + at, 16), :] = value
            dense[pl.ds(at, 16), :] = dense[pl.ds(at, 16), :] + hist[(nstep + of) % 2][(n - 1) // 2, pl.ds(at, 16), :] * here_rate
            keep(1 - of, at, value)

        sweep(of, update)

    def backward_pair(k, _):
        backward(nstep - 1 - 2 * k, 0)
        backward(nstep - 2 - 2 * k, 1)
        return 0

    lax.fori_loop(0, (nstep - 2) // 2, backward_pair, 0)
    if nstep % 2 == 1:
        backward(2, 0)
    end = fields[nstep % 2]

    def finish(at):
        image = dense[pl.ds(at, 16), :] - hist_a[0, pl.ds(at, 16), :] * end[pl.ds(edge + at, 16), :]
        dense[pl.ds(at, 16), :] = (2.0 / region[pl.ds(at, 16), :]) * image

    rows16(finish)

    for r in range(held):
        @pl.when(give_ref[r] >= 0)
        def _():
            give(r).start()

    for r in range(held):
        blank(r).wait()


def shot(aper, targets, take, give, rec_at, wavelet, pieces, sources, picks, same, observed):
    shape = pieces[0].shape
    slab = shape[1] * shape[2]
    ny, nz = shape[2:]
    cells = aper * slab
    held = give.shape[0]
    nstep, nrec = wavelet.shape[0], rec_at.shape[0]
    in_y = band(ny, CENTER_Y)
    none = np.zeros_like(in_y)
    mat_y = np.block([[in_y, in_y, none, none], [none, none, in_y, in_y]])
    in_z = band(nz, CENTER_Z)
    mat_z = np.concatenate([in_z, in_z], axis=0)
    smem = pl.BlockSpec(memory_space=pltpu.SMEM)
    vmem = pl.BlockSpec(memory_space=pltpu.VMEM)
    hbm = pl.BlockSpec(memory_space=pl.ANY)
    f32 = jnp.float32
    edge = REACH * ny
    *grads, misfit = pl.pallas_call(
        functools.partial(kernel, len(pieces), targets),
        out_shape=(
            *[jax.ShapeDtypeStruct((held // targets, slab, nz), f32)] * targets,
            jax.ShapeDtypeStruct((nrec, nstep), f32),
        ),
        in_specs=[smem] * 4 + [hbm] + [vmem] * 5 + [hbm] * len(pieces),
        out_specs=(*[hbm] * targets, vmem),
        scratch_shapes=[
            pltpu.VMEM(((nstep + 1) // 2, cells, nz), f32),
            pltpu.VMEM((nstep // 2, cells, nz), f32),
            pltpu.VMEM((cells + 2 * edge, nz), f32),
            pltpu.VMEM((cells + 2 * edge, nz), f32),
            pltpu.VMEM((cells, 2 * nz), jnp.bfloat16),
            pltpu.VMEM((cells, 2 * nz), jnp.bfloat16),
            pltpu.VMEM((GROUP * ny, nz), f32),
            pltpu.VMEM((GROUP * ny, nz), f32),
            pltpu.VMEM((cells, nz), f32),
            pltpu.VMEM((cells, nz), f32),
            pltpu.VMEM((cells, nz), f32),
            pltpu.VMEM((cells, nz), f32),
            pltpu.VMEM((nstep, nrec, nz), f32),
            pltpu.VMEM((nrec, nz), f32),
            pltpu.SemaphoreType.DMA((aper,)),
            pltpu.SemaphoreType.DMA,
            pltpu.SemaphoreType.DMA((held,)),
        ],
        compiler_params=pltpu.CompilerParams(vmem_limit_bytes=60 * 1024 * 1024),
        name="shot_gradient",
    )(
        take, give, rec_at, wavelet, sources, picks, same, observed,
        jnp.asarray(mat_y, jnp.bfloat16), jnp.asarray(mat_z, jnp.bfloat16),
        *[piece.reshape(-1, slab, nz) for piece in pieces],
    )
    return grads, misfit


SIDE_Z, SIDE_Y, SIDE_CORE = 4, 2, 2
Z_ORDER = (0, 2, 1, 3)


def place(z, y, core):
    return (z * SIDE_Y + y) * SIDE_CORE + core


def trade(block, z=0, y=0, core=0):
    flip = place(z, y, core)
    return lax.ppermute(block, "shot", [(i, i ^ flip) for i in range(SIDE_Z * SIDE_Y * SIDE_CORE)])


def collect(velocity):
    first, second = velocity[:1], velocity[1:]
    beside = trade(second, y=1)
    first = jnp.concatenate([first, trade(first, z=2)])
    second = jnp.concatenate([second, beside])
    second = jnp.concatenate([second, trade(second, z=2)])
    first = jnp.concatenate([first, trade(first, z=1)])
    pieces = [first, second, trade(first, y=1), trade(second, z=1)]
    return pieces + [trade(piece, core=1) for piece in pieces]


def collected():
    offsets = []
    for core in range(SIDE_CORE):
        offsets += [(place(a, 0, core), 0) for a in Z_ORDER]
        offsets += [(place(a, b, core), 1) for a in Z_ORDER[:2] for b in range(SIDE_Y)]
        offsets += [(place(a, 1, core), 0) for a in Z_ORDER]
        offsets += [(place(a, b, core), 1) for a in Z_ORDER[2:] for b in range(SIDE_Y)]
    return offsets


def handed():
    offsets = []
    for core in range(SIDE_CORE):
        offsets += [(place(a, b, core), 0) for b in range(SIDE_Y) for a in Z_ORDER]
        offsets += [(place(a, b, core), 1) for a in Z_ORDER for b in range(SIDE_Y)]
    return offsets


def reduce(grads):
    first, second, far_first, far_second = grads
    first = first + trade(far_first, core=1)
    second = second + trade(far_second, core=1)
    first, second = first[:4] + trade(first[4:], y=1), second[:4] + trade(second[4:], z=1)
    first, second = first[:2] + trade(first[2:], z=1), second[:2] + trade(second[2:], z=2)
    first, second = first[:1] + trade(first[1:], z=2), second[:1] + trade(second[1:], y=1)
    return jnp.concatenate([first, second])


def shards(velocity, tile_owner, aperture, source_at, source_amp, receivers, wavelet, observed):
    devices = lax.axis_size("shot")
    me = lax.axis_index("shot")
    per_dev = velocity.shape[0]
    slabs = aperture[0]
    aper = slabs.shape[0]
    nz = velocity.shape[3]
    store_rows = tile_owner[slabs] * per_dev + slabs // devices
    split = devices == SIDE_Z * SIDE_Y * SIDE_CORE and per_dev == 2
    if split:
        pieces = collect(velocity)
        taken, given = collected(), handed()
        outs = 2 * SIDE_CORE
    else:
        pieces = [lax.all_gather(velocity, "shot", axis=0, tiled=True)]
        taken = given = [(d, r) for d in range(devices) for r in range(per_dev)]
        me = 0
        outs = 1

    def slots(offsets):
        at = np.asarray(offsets, np.int32)
        rows = (me ^ at[:, 0]) * per_dev + at[:, 1]
        hit = rows[:, None] == store_rows[None, :]
        return jnp.max(jnp.where(hit, jnp.arange(aper, dtype=jnp.int32)[None, :], -1), axis=1)

    cells = aper * velocity.shape[1] * velocity.shape[2]
    sources = jnp.zeros((cells * nz,), jnp.float32).at[source_at[0]].add(source_amp[0]).reshape(cells, nz)
    rec_at = receivers[0] // nz
    lane = receivers[0] % nz
    picks = (lane[:, None] == jnp.arange(nz, dtype=jnp.int32)[None, :]).astype(jnp.float32)
    same = (rec_at[:, None] == rec_at[None, :]).astype(jnp.float32)
    grads, misfit = shot(
        aper, outs, slots(taken), slots(given), rec_at, wavelet, pieces, sources, picks, same, observed[0].T
    )
    if split:
        gradient = reduce(grads)
    else:
        gradient = lax.psum_scatter(grads[0], "shot", scatter_dimension=0, tiled=True)
    return (gradient.reshape(velocity.shape), misfit.T[None])


def solution(mesh):
    in_specs = (
        P(("groups", "shot"), None, None, None),
        P(),
        P(("groups", "shot"), None),
        P(("groups", "shot"), None),
        P(("groups", "shot"), None),
        P(("groups", "shot"), None),
        P(),
        P(("groups", "shot"), None, None),
    )
    out_specs = (P(("groups", "shot"), None, None, None), P(("groups", "shot"), None, None))
    return jax.shard_map(shards, mesh=mesh, in_specs=in_specs, out_specs=out_specs, check_vma=False)
```

time: 305 us -> 182 us (0.60)
  Pallas kernels: 163 us -> 93.4 us
  waiting for transfers between devices: 117 us -> 52.6 us
  starting transfers between devices: 0.08 us -> 19.8 us
  between operations: 14.1 us -> 0.96 us
    reduce_scatter x1 -> x0, waiting for transfers between devices: 69.6 us -> none  [shards(): gradient = lax.psum_scatter(grad, 'shot', scatter_dimension=0, tiled=True)]
    pallas_call x1, Pallas kernels: 163 us -> 93.4 us  [shot(): pl.pallas_call(functools.partial(kernel, len(pieces), targets), out_shape...]
    ppermute x0 -> x18, waiting for transfers between devices: none -> 52.6 us  [trade(): lax.ppermute(block, 'shot', [(i, i ^ flip) for i in range(SIDE_Z * SIDE_Y...]
    all_gather x1 -> x0, waiting for transfers between devices: 46.6 us -> none  [shards(): pieces = lax.all_gather(velocity, 'shot', axis=0, tiled=True)]
    ppermute x0 -> x18, starting transfers between devices: none -> 19.8 us  [trade(): lax.ppermute(block, 'shot', [(i, i ^ flip) for i in range(SIDE_Z * SIDE_Y...]
  transfers between devices with their start and end apart: 2 -> 18, of which waited for: 2 -> 12; matrix products, arithmetic and copies ran while one was open for 3% -> 7% of each run, Pallas kernels for 0% -> 0%
where the time goes in v2:
time: 182 us; the launch traced here: 181 us
  Pallas kernels  93.4 us (51%)
  waiting for transfers between devices  52.6 us (29%)
  starting transfers between devices  19.8 us (11%)
  other arithmetic  9.7 us (5%)
  local copies, waits for them, and re-layouts  4.92 us (3%)
    pallas_call x1, Pallas kernels, shot(): pl.pallas_call(functools.partial(kernel, len(pieces), targets), out_shape...  93.4 us
    ppermute x18, waiting for transfers between devices, trade(): lax.ppermute(block, 'shot', [(i, i ^ flip) for i in range(SIDE_Z * SIDE_Y...  52.6 us
    ppermute x18, starting transfers between devices, trade(): lax.ppermute(block, 'shot', [(i, i ^ flip) for i in range(SIDE_Z * SIDE_Y...  19.8 us
  transfers between devices with their start and end apart: 18, of which 12 were waited for; matrix products, arithmetic and copies ran while one was open for 7% of the time, Pallas kernels for 0%

profile of v2, /device:TPU:0, one launch (start us, length us, event | category | flops | bytes accessed | tf_op | source)
XLA Modules:
  0.0 181.4 jit_solution(14029881364490963968)
XLA Ops:
  0.6 0.0 copy-start
  0.6 1.0 fusion.6
  1.6 3.0 %collective-permute-start.2 = (f32[1,4,64,128]{3,2,1,0:T(8,128)S(1)}, f32[1,4,64,128]{3,2,1,0:T(8,128)S(1)}, u32[]{:S(2)}, u32[]{:S(2)}) collective-permute-start(f32[1,4,64,128]{3,2,1,0:T(8,128)S(1)} %get-tuple-element.20), channel_id=1, source_target_pairs={{0,2},{1,3},{2,0},{3,1},{4,6},{5,7},{6,4},{7,5},{8,10},{9,11},{10,... | collective-permute-start | bytes 393224 | tf_op jit(solution)/shard_map/ppermute | solution.py:348
  4.7 2.6 %collective-permute-start = (f32[1,4,64,128]{3,2,1,0:T(8,128)S(1)}, f32[1,4,64,128]{3,2,1,0:T(8,128)S(1)}, u32[]{:S(2)}, u32[]{:S(2)}) collective-permute-start(f32[1,4,64,128]{3,2,1,0:T(8,128)S(1)} %get-tuple-element.21), channel_id=1, source_target_pairs={{0,8},{1,9},{2,10},{3,11},{4,12},{5,13},{6,14},{7,15},{8,0},{9,1},... | collective-permute-start | bytes 393224 | tf_op jit(solution)/shard_map/ppermute | solution.py:348
  7.3 0.7 compare_select_fusion
  7.9 0.7 fusion.3
  8.6 1.4 copy.20
  10.0 3.3 %collective-permute-done = f32[1,4,64,128]{3,2,1,0:T(8,128)S(1)} collective-permute-done((f32[1,4,64,128]{3,2,1,0:T(8,128)S(1)}, f32[1,4,64,128]{3,2,1,0:T(8,128)S(1)}, u32[]{:S(2)}, u32[]{:S(2)}) %collective-permute-start) | collective-permute-done | bytes 131104 | tf_op jit(solution)/shard_map/ppermute | solution.py:348
  13.4 0.7 collective-permute-start.1
  14.1 0.0 collective-permute-done.2
  14.1 3.4 %collective-permute-start.3 = (f32[2,4,64,128]{3,2,1,0:T(8,128)S(1)}, f32[2,4,64,128]{3,2,1,0:T(8,128)S(1)}, u32[]{:S(2)}, u32[]{:S(2)}) collective-permute-start(f32[2,4,64,128]{3,2,1,0:T(8,128)S(1)} %pad_maximum_fusion.3), channel_id=1, source_target_pairs={{0,8},{1,9},{2,10},{3,11},{4,12},{5,13},{6,14},{7,15},{8,0},{9,1},... | collective-permute-start | bytes 786440 | tf_op jit(solution)/shard_map/ppermute | solution.py:348
  17.6 0.7 fusion.5
  18.2 7.7 %collective-permute-done.1 = f32[2,4,64,128]{3,2,1,0:T(8,128)S(1)} collective-permute-done((f32[2,4,64,128]{3,2,1,0:T(8,128)S(1)}, f32[2,4,64,128]{3,2,1,0:T(8,128)S(1)}, u32[]{:S(2)}, u32[]{:S(2)}) %collective-permute-start.1) | collective-permute-done | bytes 262176 | tf_op jit(solution)/shard_map/ppermute | solution.py:348
  25.9 0.0 copy-start.16
  26.0 0.0 copy-start.12
  26.0 0.0 copy-start.13
  26.0 0.0 copy-start.14
  26.0 0.0 copy-start.15
  26.0 0.0 copy-start.17
  26.0 0.6 collective-permute-start.4
  26.6 2.8 %collective-permute-done.3 = f32[2,4,64,128]{3,2,1,0:T(8,128)S(1)} collective-permute-done((f32[2,4,64,128]{3,2,1,0:T(8,128)S(1)}, f32[2,4,64,128]{3,2,1,0:T(8,128)S(1)}, u32[]{:S(2)}, u32[]{:S(2)}) %collective-permute-start.3) | collective-permute-done | bytes 262176 | tf_op jit(solution)/shard_map/ppermute | solution.py:348
  29.5 0.3 collective-permute-start.5
  29.8 0.7 gather_fusion
  30.5 3.6 %scatter_custom_fusion = f32[524288]{0:T(1024)} fusion(s32[256]{0:T(256)S(1)} %bitcast.59, f32[256]{0:T(256)} %bitcast.60, f32[]{:T(128)} %constant.68.clone.1), kind=kCustom, calls=%fused_computation.2 | custom fusion | flops 256 | bytes 2097664 | tf_op jit(solution)/shard_map/scatter-add | solution.py:416
  34.0 0.0 copy-done.16
  34.1 0.1 collective-permute-start.6
  34.2 0.5 collective-permute-start.7
  34.7 2.8 %collective-permute-done.4 = f32[4,4,64,128]{3,2,1,0:T(8,128)S(1)} collective-permute-done((f32[4,4,64,128]{3,2,1,0:T(8,128)S(1)}, f32[4,4,64,128]{3,2,1,0:T(8,128)S(1)}, u32[]{:S(2)}, u32[]{:S(2)}) %collective-permute-start.4) | collective-permute-done | bytes 524320 | tf_op jit(solution)/shard_map/ppermute | solution.py:348
  37.5 0.0 collective-permute-start.8
  37.5 3.8 %collective-permute-done.5 = f32[4,4,64,128]{3,2,1,0:T(8,128)S(1)} collective-permute-done((f32[4,4,64,128]{3,2,1,0:T(8,128)S(1)}, f32[4,4,64,128]{3,2,1,0:T(8,128)S(1)}, u32[]{:S(2)}, u32[]{:S(2)}) %collective-permute-start.5) | collective-permute-done | bytes 524320 | tf_op jit(solution)/shard_map/ppermute | solution.py:348
  41.3 0.0 collective-permute-start.9
  41.3 0.7 select_reduce_fusion
  42.1 0.8 fusion.2
  42.8 0.0 collective-permute-done.6
  42.8 0.0 collective-permute-done.7
  42.8 0.0 collective-permute-done.8
  42.9 0.0 copy-start.8
  42.9 0.4 collective-permute-done.9
  43.2 1.0 copy-done.9
  44.2 0.0 copy-done.2
  44.2 93.4 %shot_gradient.1 = (f32[8,256,128]{2,1,0:T(8,128)}, f32[8,256,128]{2,1,0:T(8,128)}, f32[8,256,128]{2,1,0:T(8,128)}, f32[8,256,128]{2,1,0:T(8,128)}, f32[128,16]{1,0:T(8,128)}) custom-call(s32[32]{0:T(128)} %get-tuple-element.19.take_ref, s32[32]{0:T(128)} %get-tuple-element.18.give_ref, s32[128]{0:T(128)} %copy-done.11, f32[16]{0:T(128)} %wav_ref.1, ...), custom_call_target="tpu_custom_call" | custom-call | tf_op jit(solution)/shard_map/shot_gradient/pallas_call | solution.py:301
  137.7 0.4 collective-permute-start.10
  138.1 0.1 collective-permute-start.14
  138.2 2.4 %collective-permute-done.10 = f32[8,256,128]{2,1,0:T(8,128)S(1)} collective-permute-done((f32[8,256,128]{2,1,0:T(8,128)}, f32[8,256,128]{2,1,0:T(8,128)S(1)}, u32[]{:S(2)}, u32[]{:S(2)}) %collective-permute-start.10) | collective-permute-done | bytes 1048608 | tf_op jit(solution)/shard_map/ppermute | solution.py:348
  140.6 1.5 add.84
  142.1 0.6 collective-permute-start.11
  142.7 0.0 collective-permute-done.14
  142.7 0.1 add.88
  142.9 1.8 collective-permute-start.15
  144.6 11.8 %collective-permute-done.11 = f32[4,256,128]{2,1,0:T(8,128)S(1)} collective-permute-done((f32[4,256,128]{2,1,0:T(8,128)S(1)}, f32[4,256,128]{2,1,0:T(8,128)S(1)}, u32[]{:S(2)}, u32[]{:S(2)}) %collective-permute-start.11) | collective-permute-done | bytes 524320 | tf_op jit(solution)/shard_map/ppermute | solution.py:348
  156.4 0.1 slice_add_fusion.1
  156.5 1.7 collective-permute-start.12
  158.2 0.0 collective-permute-done.15
  158.2 0.1 slice_add_fusion
  158.3 2.5 %collective-permute-start.16 = (f32[2,256,128]{2,1,0:T(8,128)S(1)}, f32[2,256,128]{2,1,0:T(8,128)S(1)}, u32[]{:S(2)}, u32[]{:S(2)}) collective-permute-start(f32[2,256,128]{2,1,0:T(8,128)S(1)} %slice.67), channel_id=1, source_target_pairs={{0,8},{1,9},{2,10},{3,11},{4,12},{5,13},{6,14},{7,15},{8,0},{9,1},... | collective-permute-start | bytes 786440 | tf_op jit(solution)/shard_map/ppermute | solution.py:348
  160.8 0.0 copy-done.10
  160.8 0.7 copy.21
  161.4 8.0 %collective-permute-done.12 = f32[2,256,128]{2,1,0:T(8,128)S(1)} collective-permute-done((f32[2,256,128]{2,1,0:T(8,128)S(1)}, f32[2,256,128]{2,1,0:T(8,128)S(1)}, u32[]{:S(2)}, u32[]{:S(2)}) %collective-permute-start.12) | collective-permute-done | bytes 262176 | tf_op jit(solution)/shard_map/ppermute | solution.py:348
  169.5 0.9 collective-permute-start.13
  170.4 5.2 %collective-permute-done.16 = f32[2,256,128]{2,1,0:T(8,128)S(1)} collective-permute-done((f32[2,256,128]{2,1,0:T(8,128)S(1)}, f32[2,256,128]{2,1,0:T(8,128)S(1)}, u32[]{:S(2)}, u32[]{:S(2)}) %collective-permute-start.16) | collective-permute-done | bytes 262176 | tf_op jit(solution)/shard_map/ppermute | solution.py:348
  175.7 0.6 collective-permute-start.17
  176.3 1.7 collective-permute-done.13
  178.0 2.7 %collective-permute-done.17 = f32[1,256,128]{2,1,0:T(8,128)S(1)} collective-permute-done((f32[1,256,128]{2,1,0:T(8,128)S(1)}, f32[1,256,128]{2,1,0:T(8,128)S(1)}, u32[]{:S(2)}, u32[]{:S(2)}) %collective-permute-start.17) | collective-permute-done | bytes 131104 | tf_op jit(solution)/shard_map/ppermute | solution.py:348
  180.7 0.7 pad_maximum_fusion.4
  (42 shorter events, 0.4 us)
Async XLA Ops:
  0.6 29.2 %copy-start = (s32[32]{0:T(128)S(1)}, s32[32]{0:T(128)}, u32[]{:S(2)}) copy-start(s32[32]{0:T(128)} %param.15) | copy-start | bytes 388
  1.6 12.5 %collective-permute-start.2 = (f32[1,4,64,128]{3,2,1,0:T(8,128)S(1)}, f32[1,4,64,128]{3,2,1,0:T(8,128)S(1)}, u32[]{:S(2)}, u32[]{:S(2)}) collective-permute-start(f32[1,4,64,128]{3,2,1,0:T(8,128)S(1)} %get-tuple-element.20), channel_id=1, source_target_pairs={{0,2},{1,3},{2,0},{3,1},{4,6},{5,7},{6,4},{7,5},{8,10},{9,11},{10,... | collective-permute-start | bytes 393224 | tf_op jit(solution)/shard_map/ppermute | solution.py:348
  4.7 8.7 %collective-permute-start = (f32[1,4,64,128]{3,2,1,0:T(8,128)S(1)}, f32[1,4,64,128]{3,2,1,0:T(8,128)S(1)}, u32[]{:S(2)}, u32[]{:S(2)}) collective-permute-start(f32[1,4,64,128]{3,2,1,0:T(8,128)S(1)} %get-tuple-element.21), channel_id=1, source_target_pairs={{0,8},{1,9},{2,10},{3,11},{4,12},{5,13},{6,14},{7,15},{8,0},{9,1},... | collective-permute-start | bytes 393224 | tf_op jit(solution)/shard_map/ppermute | solution.py:348
  13.4 12.5 %collective-permute-start.1 = (f32[2,4,64,128]{3,2,1,0:T(8,128)S(1)}, f32[2,4,64,128]{3,2,1,0:T(8,128)S(1)}, u32[]{:S(2)}, u32[]{:S(2)}) collective-permute-start(f32[2,4,64,128]{3,2,1,0:T(8,128)S(1)} %pad_maximum_fusion.2), channel_id=1, source_target_pairs={{0,4},{1,5},{2,6},{3,7},{4,0},{5,1},{6,2},{7,3},{8,12},{9,13},{10,... | collective-permute-start | bytes 786440 | tf_op jit(solution)/shard_map/ppermute | solution.py:348
  14.1 15.3 %collective-permute-start.3 = (f32[2,4,64,128]{3,2,1,0:T(8,128)S(1)}, f32[2,4,64,128]{3,2,1,0:T(8,128)S(1)}, u32[]{:S(2)}, u32[]{:S(2)}) collective-permute-start(f32[2,4,64,128]{3,2,1,0:T(8,128)S(1)} %pad_maximum_fusion.3), channel_id=1, source_target_pairs={{0,8},{1,9},{2,10},{3,11},{4,12},{5,13},{6,14},{7,15},{8,0},{9,1},... | collective-permute-start | bytes 786440 | tf_op jit(solution)/shard_map/ppermute | solution.py:348
  25.9 18.3 %copy-start.1 = (f32[4,4,64,128]{3,2,1,0:T(8,128)}, f32[4,4,64,128]{3,2,1,0:T(8,128)S(1)}, u32[]{:S(2)}) copy-start(f32[4,4,64,128]{3,2,1,0:T(8,128)S(1)} %pad_maximum_fusion) | copy-start | bytes 1572868
  25.9 8.1 %copy-start.16 = (s32[1,16]{1,0:T(1,128)S(1)}, s32[1,16]{1,0:T(1,128)}, u32[]{:S(2)}) copy-start(s32[1,16]{1,0:T(1,128)} %param.16) | copy-start | bytes 196
  26.0 8.1 %copy-start.12 = (s32[32]{0:T(128)S(1)}, s32[32]{0:T(128)}, u32[]{:S(2)}) copy-start(s32[32]{0:T(128)} %constant.74.clone) | copy-start | bytes 388
  26.0 8.1 %copy-start.13 = (s32[32]{0:T(128)S(1)}, s32[32]{0:T(128)}, u32[]{:S(2)}) copy-start(s32[32]{0:T(128)} %constant.73.clone) | copy-start | bytes 388
  26.0 8.1 %copy-start.14 = (s32[32]{0:T(128)S(1)}, s32[32]{0:T(128)}, u32[]{:S(2)}) copy-start(s32[32]{0:T(128)} %constant.72.clone) | copy-start | bytes 388
  26.0 8.1 %copy-start.15 = (s32[32]{0:T(128)S(1)}, s32[32]{0:T(128)}, u32[]{:S(2)}) copy-start(s32[32]{0:T(128)} %constant.71.clone) | copy-start | bytes 388
  26.0 16.0 %copy-start.17 = (s32[1,128]{1,0:T(1,128)S(1)}, s32[1,128]{1,0:T(1,128)}, u32[]{:S(2)}) copy-start(s32[1,128]{1,0:T(1,128)} %param.19) | copy-start | bytes 1540
  26.0 11.5 %collective-permute-start.4 = (f32[4,4,64,128]{3,2,1,0:T(8,128)S(1)}, f32[4,4,64,128]{3,2,1,0:T(8,128)S(1)}, u32[]{:S(2)}, u32[]{:S(2)}) collective-permute-start(f32[4,4,64,128]{3,2,1,0:T(8,128)S(1)} %pad_maximum_fusion), channel_id=1, source_target_pairs={{0,2},{1,3},{2,0},{3,1},{4,6},{5,7},{6,4},{7,5},{8,10},{9,11},{10,... | collective-permute-start | bytes 1572872 | tf_op jit(solution)/shard_map/ppermute | solution.py:348
  29.5 14.7 %copy-start.2 = (f32[4,4,64,128]{3,2,1,0:T(8,128)}, f32[4,4,64,128]{3,2,1,0:T(8,128)S(1)}, u32[]{:S(2)}) copy-start(f32[4,4,64,128]{3,2,1,0:T(8,128)S(1)} %pad_maximum_fusion.1) | copy-start | bytes 1572868
  29.5 11.8 %collective-permute-start.5 = (f32[4,4,64,128]{3,2,1,0:T(8,128)S(1)}, f32[4,4,64,128]{3,2,1,0:T(8,128)S(1)}, u32[]{:S(2)}, u32[]{:S(2)}) collective-permute-start(f32[4,4,64,128]{3,2,1,0:T(8,128)S(1)} %pad_maximum_fusion.1), channel_id=1, source_target_pairs={{0,4},{1,5},{2,6},{3,7},{4,0},{5,1},{6,2},{7,3},{8,12},{9,13},{10,... | collective-permute-start | bytes 1572872 | tf_op jit(solution)/shard_map/ppermute | solution.py:348
  34.1 8.7 %collective-permute-start.6 = (f32[4,4,64,128]{3,2,1,0:T(8,128)S(1)}, f32[4,4,64,128]{3,2,1,0:T(8,128)S(1)}, u32[]{:S(2)}, u32[]{:S(2)}) collective-permute-start(f32[4,4,64,128]{3,2,1,0:T(8,128)S(1)} %pad_maximum_fusion), channel_id=1, source_target_pairs={{0,1},{1,0},{2,3},{3,2},{4,5},{5,4},{6,7},{7,6},{8,9},{9,8},{10,11... | collective-permute-start | bytes 1572872 | tf_op jit(solution)/shard_map/ppermute | solution.py:348
  34.2 8.7 %collective-permute-start.7 = (f32[4,4,64,128]{3,2,1,0:T(8,128)S(1)}, f32[4,4,64,128]{3,2,1,0:T(8,128)S(1)}, u32[]{:S(2)}, u32[]{:S(2)}) collective-permute-start(f32[4,4,64,128]{3,2,1,0:T(8,128)S(1)} %pad_maximum_fusion.1), channel_id=1, source_target_pairs={{0,1},{1,0},{2,3},{3,2},{4,5},{5,4},{6,7},{7,6},{8,9},{9,8},{10,11... | collective-permute-start | bytes 1572872 | tf_op jit(solution)/shard_map/ppermute | solution.py:348
  37.5 6.7 %copy-start.4 = (f32[4,4,64,128]{3,2,1,0:T(8,128)}, f32[4,4,64,128]{3,2,1,0:T(8,128)S(1)}, u32[]{:S(2)}) copy-start(f32[4,4,64,128]{3,2,1,0:T(8,128)S(1)} %collective-permute-done.4) | copy-start | bytes 1572868
  37.5 5.3 %collective-permute-start.8 = (f32[4,4,64,128]{3,2,1,0:T(8,128)S(1)}, f32[4,4,64,128]{3,2,1,0:T(8,128)S(1)}, u32[]{:S(2)}, u32[]{:S(2)}) collective-permute-start(f32[4,4,64,128]{3,2,1,0:T(8,128)S(1)} %collective-permute-done.4), channel_id=1, source_target_pairs={{0,1},{1,0},{2,3},{3,2},{4,5},{5,4},{6,7},{7,6},{8,9},{9,8},{10,11... | collective-permute-start | bytes 1572872 | tf_op jit(solution)/shard_map/ppermute | solution.py:348
  41.3 2.9 %copy-start.5 = (f32[4,4,64,128]{3,2,1,0:T(8,128)}, f32[4,4,64,128]{3,2,1,0:T(8,128)S(1)}, u32[]{:S(2)}) copy-start(f32[4,4,64,128]{3,2,1,0:T(8,128)S(1)} %collective-permute-done.5) | copy-start | bytes 1572868
  41.3 1.9 %collective-permute-start.9 = (f32[4,4,64,128]{3,2,1,0:T(8,128)S(1)}, f32[4,4,64,128]{3,2,1,0:T(8,128)S(1)}, u32[]{:S(2)}, u32[]{:S(2)}) collective-permute-start(f32[4,4,64,128]{3,2,1,0:T(8,128)S(1)} %collective-permute-done.5), channel_id=1, source_target_pairs={{0,1},{1,0},{2,3},{3,2},{4,5},{5,4},{6,7},{7,6},{8,9},{9,8},{10,11... | collective-permute-start | bytes 1572872 | tf_op jit(solution)/shard_map/ppermute | solution.py:348
  42.1 2.1 %copy-start.11 = (s32[128]{0:T(128)}, s32[128]{0:T(128)S(1)}, u32[]{:S(2)}) copy-start(s32[128]{0:T(128)S(1)} %get-tuple-element.23.rec_ref) | copy-start | bytes 1540
  42.8 1.4 copy-start.6
  42.8 1.4 copy-start.7
  42.9 1.4 copy-start.8
  43.2 1.0 copy-start.9
  137.7 2.9 %collective-permute-start.10 = (f32[8,256,128]{2,1,0:T(8,128)}, f32[8,256,128]{2,1,0:T(8,128)S(1)}, u32[]{:S(2)}, u32[]{:S(2)}) collective-permute-start(f32[8,256,128]{2,1,0:T(8,128)} %get-tuple-element.8), channel_id=1, source_target_pairs={{0,1},{1,0},{2,3},{3,2},{4,5},{5,4},{6,7},{7,6},{8,9},{9,8},{10,11... | collective-permute-start | bytes 3145736 | tf_op jit(solution)/shard_map/ppermute | solution.py:348
  138.1 4.6 %collective-permute-start.14 = (f32[8,256,128]{2,1,0:T(8,128)}, f32[8,256,128]{2,1,0:T(8,128)S(1)}, u32[]{:S(2)}, u32[]{:S(2)}) collective-permute-start(f32[8,256,128]{2,1,0:T(8,128)} %get-tuple-element.10), channel_id=1, source_target_pairs={{0,1},{1,0},{2,3},{3,2},{4,5},{5,4},{6,7},{7,6},{8,9},{9,8},{10,11... | collective-permute-start | bytes 3145736 | tf_op jit(solution)/shard_map/ppermute | solution.py:348
  140.6 2.1 %copy-start.3 = (f32[8,256,128]{2,1,0:T(8,128)S(1)}, f32[8,256,128]{2,1,0:T(8,128)}, u32[]{:S(2)}) copy-start(f32[8,256,128]{2,1,0:T(8,128)} %get-tuple-element.9) | copy-start | bytes 3145732
  142.1 14.3 %collective-permute-start.11 = (f32[4,256,128]{2,1,0:T(8,128)S(1)}, f32[4,256,128]{2,1,0:T(8,128)S(1)}, u32[]{:S(2)}, u32[]{:S(2)}) collective-permute-start(f32[4,256,128]{2,1,0:T(8,128)S(1)} %slice.59), channel_id=1, source_target_pairs={{0,2},{1,3},{2,0},{3,1},{4,6},{5,7},{6,4},{7,5},{8,10},{9,11},{10,... | collective-permute-start | bytes 1572872 | tf_op jit(solution)/shard_map/ppermute | solution.py:348
  142.9 17.9 %copy-start.10 = (f32[128,16]{1,0:T(8,128)S(1)}, f32[128,16]{1,0:T(8,128)}, u32[]{:S(2)}) copy-start(f32[128,16]{1,0:T(8,128)} %get-tuple-element.11) | copy-start | bytes 24580
  142.9 15.3 %collective-permute-start.15 = (f32[4,256,128]{2,1,0:T(8,128)S(1)}, f32[4,256,128]{2,1,0:T(8,128)S(1)}, u32[]{:S(2)}, u32[]{:S(2)}) collective-permute-start(f32[4,256,128]{2,1,0:T(8,128)S(1)} %slice.65), channel_id=1, source_target_pairs={{0,4},{1,5},{2,6},{3,7},{4,0},{5,1},{6,2},{7,3},{8,12},{9,13},{10,... | collective-permute-start | bytes 1572872 | tf_op jit(solution)/shard_map/ppermute | solution.py:348
  156.5 13.0 %collective-permute-start.12 = (f32[2,256,128]{2,1,0:T(8,128)S(1)}, f32[2,256,128]{2,1,0:T(8,128)S(1)}, u32[]{:S(2)}, u32[]{:S(2)}) collective-permute-start(f32[2,256,128]{2,1,0:T(8,128)S(1)} %slice.61), channel_id=1, source_target_pairs={{0,4},{1,5},{2,6},{3,7},{4,0},{5,1},{6,2},{7,3},{8,12},{9,13},{10,... | collective-permute-start | bytes 786440 | tf_op jit(solution)/shard_map/ppermute | solution.py:348
  158.3 17.3 %collective-permute-start.16 = (f32[2,256,128]{2,1,0:T(8,128)S(1)}, f32[2,256,128]{2,1,0:T(8,128)S(1)}, u32[]{:S(2)}, u32[]{:S(2)}) collective-permute-start(f32[2,256,128]{2,1,0:T(8,128)S(1)} %slice.67), channel_id=1, source_target_pairs={{0,8},{1,9},{2,10},{3,11},{4,12},{5,13},{6,14},{7,15},{8,0},{9,1},... | collective-permute-start | bytes 786440 | tf_op jit(solution)/shard_map/ppermute | solution.py:348
  169.5 8.5 %collective-permute-start.13 = (f32[1,256,128]{2,1,0:T(8,128)S(1)}, f32[1,256,128]{2,1,0:T(8,128)S(1)}, u32[]{:S(2)}, u32[]{:S(2)}) collective-permute-start(f32[1,256,128]{2,1,0:T(8,128)S(1)} %slice.63), channel_id=1, source_target_pairs={{0,8},{1,9},{2,10},{3,11},{4,12},{5,13},{6,14},{7,15},{8,0},{9,1},... | collective-permute-start | bytes 393224 | tf_op jit(solution)/shard_map/ppermute | solution.py:348
  175.7 5.0 %collective-permute-start.17 = (f32[1,256,128]{2,1,0:T(8,128)S(1)}, f32[1,256,128]{2,1,0:T(8,128)S(1)}, u32[]{:S(2)}, u32[]{:S(2)}) collective-permute-start(f32[1,256,128]{2,1,0:T(8,128)S(1)} %slice.69), channel_id=1, source_target_pairs={{0,2},{1,3},{2,0},{3,1},{4,6},{5,7},{6,4},{7,5},{8,10},{9,11},{10,... | collective-permute-start | bytes 393224 | tf_op jit(solution)/shard_map/ppermute | solution.py:348

commit v3 on v2

--- a/solution.py
+++ b/solution.py
@@ -98,7 +98,7 @@
             rec_rows[n, pl.ds(r, 1), :] = fields[to][pl.ds(edge + rec_ref[r], 1), :]
             return 0
 
-        lax.fori_loop(0, nrec, body, 0, unroll=16)
+        lax.fori_loop(0, nrec, body, 0, unroll=64)
 
     def multiply(base, of, taps):
         both = halves[of][pl.ds(base, block), :]
@@ -140,7 +140,7 @@
             combine(base + block, of, taps_b, update)
             return 0
 
-        lax.fori_loop(0, groups // 2 - 1, body, 0)
+        lax.fori_loop(0, groups // 2 - 1, body, 0, unroll=True)
         base = (groups - 2) * block
         multiply(base + block, of, taps_b)
         combine(base, of, taps_a, update)
@@ -152,7 +152,7 @@
             fn(pl.multiple_of(g * 16, 16))
             return 0
 
-        lax.fori_loop(0, cells // 16, body, 0, unroll=4)
+        lax.fori_loop(0, cells // 16, body, 0, unroll=16)
 
     source.wait()
 
@@ -211,7 +211,9 @@
         )
         return total
 
-    records = lax.fori_loop(0, nstep, compare, jnp.zeros((nrec, nstep), jnp.float32))
+    records = jnp.zeros((nrec, nstep), jnp.float32)
+    for n in range(nstep):
+        records = compare(n, records)
     mis_ref[...] = records - obs_ref[...]
 
     def inject(n):
@@ -219,14 +221,14 @@
             moved[pl.ds(r, 1), :] = rate[pl.ds(rec_ref[r], 1), :]
             return 0
 
-        lax.fori_loop(0, nrec, take, 0, unroll=16)
+        lax.fori_loop(0, nrec, take, 0, unroll=64)
         moved[...] = moved[...] + rec_rows[n]
 
         def put(r, _):
             rate[pl.ds(rec_ref[r], 1), :] = moved[pl.ds(r, 1), :]
             return 0
 
-        lax.fori_loop(0, nrec, put, 0, unroll=16)
+        lax.fori_loop(0, nrec, put, 0, unroll=64)
 
     def clear(at):
         rate[pl.ds(at, 16), :] = jnp.zeros((16, LANES), jnp.float32)

time: 182 us -> 171 us (0.940)
  Pallas kernels: 93.4 us -> 82.4 us
    pallas_call x1, Pallas kernels: 93.4 us -> 82.4 us  [shot(): pl.pallas_call(functools.partial(kernel, len(pieces), targets), out_shape...]
where the time goes in v3:
time: 171 us
  Pallas kernels  82.4 us (48%)
  waiting for transfers between devices  52.4 us (31%)
  starting transfers between devices  20.3 us (12%)
  other arithmetic  9.7 us (6%)
  local copies, waits for them, and re-layouts  4.91 us (3%)
    pallas_call x1, Pallas kernels, shot(): pl.pallas_call(functools.partial(kernel, len(pieces), targets), out_shape...  82.4 us
    ppermute x18, waiting for transfers between devices, trade(): lax.ppermute(block, 'shot', [(i, i ^ flip) for i in range(SIDE_Z * SIDE_Y...  52.4 us
    ppermute x18, starting transfers between devices, trade(): lax.ppermute(block, 'shot', [(i, i ^ flip) for i in range(SIDE_Z * SIDE_Y...  20.3 us
    scatter-add x1, other arithmetic, shards(): jnp.zeros((cells * nz,), jnp.float32).at[source_at[0]].add(source_amp[0])  3.55 us
  transfers between devices with their start and end apart: 18, of which 12 were waited for; matrix products, arithmetic and copies ran while one was open for 7% of the time, Pallas kernels for 0%

profile of v3, /device:TPU:0, one launch (start us, length us, event | category | flops | bytes accessed | tf_op | source)
XLA Modules:
  0.0 170.6 jit_solution(11680141493650871345)
XLA Ops:
  0.6 0.0 copy-start
  0.6 1.0 fusion.6
  1.6 3.0 %collective-permute-start.2 = (f32[1,4,64,128]{3,2,1,0:T(8,128)S(1)}, f32[1,4,64,128]{3,2,1,0:T(8,128)S(1)}, u32[]{:S(2)}, u32[]{:S(2)}) collective-permute-start(f32[1,4,64,128]{3,2,1,0:T(8,128)S(1)} %get-tuple-element.20), channel_id=1, source_target_pairs={{0,2},{1,3},{2,0},{3,1},{4,6},{5,7},{6,4},{7,5},{8,10},{9,11},{10,... | collective-permute-start | bytes 393224 | tf_op jit(solution)/shard_map/ppermute | solution.py:350
  4.7 2.6 %collective-permute-start = (f32[1,4,64,128]{3,2,1,0:T(8,128)S(1)}, f32[1,4,64,128]{3,2,1,0:T(8,128)S(1)}, u32[]{:S(2)}, u32[]{:S(2)}) collective-permute-start(f32[1,4,64,128]{3,2,1,0:T(8,128)S(1)} %get-tuple-element.21), channel_id=1, source_target_pairs={{0,8},{1,9},{2,10},{3,11},{4,12},{5,13},{6,14},{7,15},{8,0},{9,1},... | collective-permute-start | bytes 393224 | tf_op jit(solution)/shard_map/ppermute | solution.py:350
  7.3 0.7 compare_select_fusion
  7.9 0.7 fusion.3
  8.6 1.4 copy.20
  10.0 3.3 %collective-permute-done = f32[1,4,64,128]{3,2,1,0:T(8,128)S(1)} collective-permute-done((f32[1,4,64,128]{3,2,1,0:T(8,128)S(1)}, f32[1,4,64,128]{3,2,1,0:T(8,128)S(1)}, u32[]{:S(2)}, u32[]{:S(2)}) %collective-permute-start) | collective-permute-done | bytes 131104 | tf_op jit(solution)/shard_map/ppermute | solution.py:350
  13.4 0.7 collective-permute-start.1
  14.1 0.0 collective-permute-done.2
  14.1 3.4 %collective-permute-start.3 = (f32[2,4,64,128]{3,2,1,0:T(8,128)S(1)}, f32[2,4,64,128]{3,2,1,0:T(8,128)S(1)}, u32[]{:S(2)}, u32[]{:S(2)}) collective-permute-start(f32[2,4,64,128]{3,2,1,0:T(8,128)S(1)} %pad_maximum_fusion.3), channel_id=1, source_target_pairs={{0,8},{1,9},{2,10},{3,11},{4,12},{5,13},{6,14},{7,15},{8,0},{9,1},... | collective-permute-start | bytes 786440 | tf_op jit(solution)/shard_map/ppermute | solution.py:350
  17.6 0.7 fusion.5
  18.2 7.7 %collective-permute-done.1 = f32[2,4,64,128]{3,2,1,0:T(8,128)S(1)} collective-permute-done((f32[2,4,64,128]{3,2,1,0:T(8,128)S(1)}, f32[2,4,64,128]{3,2,1,0:T(8,128)S(1)}, u32[]{:S(2)}, u32[]{:S(2)}) %collective-permute-start.1) | collective-permute-done | bytes 262176 | tf_op jit(solution)/shard_map/ppermute | solution.py:350
  25.9 0.0 copy-start.1
  25.9 0.0 copy-start.16
  26.0 0.0 copy-start.12
  26.0 0.0 copy-start.13
  26.0 0.0 copy-start.14
  26.0 0.0 copy-start.15
  26.0 0.0 copy-start.17
  26.0 0.6 collective-permute-start.4
  26.6 2.8 %collective-permute-done.3 = f32[2,4,64,128]{3,2,1,0:T(8,128)S(1)} collective-permute-done((f32[2,4,64,128]{3,2,1,0:T(8,128)S(1)}, f32[2,4,64,128]{3,2,1,0:T(8,128)S(1)}, u32[]{:S(2)}, u32[]{:S(2)}) %collective-permute-start.3) | collective-permute-done | bytes 262176 | tf_op jit(solution)/shard_map/ppermute | solution.py:350
  29.5 0.3 collective-permute-start.5
  29.8 0.0 copy-done
  29.8 0.7 gather_fusion
  30.5 3.6 %scatter_custom_fusion = f32[524288]{0:T(1024)} fusion(s32[256]{0:T(256)S(1)} %bitcast.59, f32[256]{0:T(256)} %bitcast.60, f32[]{:T(128)} %constant.68.clone.1), kind=kCustom, calls=%fused_computation.2 | custom fusion | flops 256 | bytes 2097664 | tf_op jit(solution)/shard_map/scatter-add | solution.py:418
  34.1 0.1 collective-permute-start.6
  34.2 0.5 collective-permute-start.7
  34.7 2.8 %collective-permute-done.4 = f32[4,4,64,128]{3,2,1,0:T(8,128)S(1)} collective-permute-done((f32[4,4,64,128]{3,2,1,0:T(8,128)S(1)}, f32[4,4,64,128]{3,2,1,0:T(8,128)S(1)}, u32[]{:S(2)}, u32[]{:S(2)}) %collective-permute-start.4) | collective-permute-done | bytes 524320 | tf_op jit(solution)/shard_map/ppermute | solution.py:350
  37.5 0.0 collective-permute-start.8
  37.5 3.8 %collective-permute-done.5 = f32[4,4,64,128]{3,2,1,0:T(8,128)S(1)} collective-permute-done((f32[4,4,64,128]{3,2,1,0:T(8,128)S(1)}, f32[4,4,64,128]{3,2,1,0:T(8,128)S(1)}, u32[]{:S(2)}, u32[]{:S(2)}) %collective-permute-start.5) | collective-permute-done | bytes 524320 | tf_op jit(solution)/shard_map/ppermute | solution.py:350
  41.3 0.0 collective-permute-start.9
  41.3 0.7 select_reduce_fusion
  42.0 0.0 copy-done.17
  42.1 0.0 copy-start.11
  42.1 0.8 fusion.2
  42.8 0.0 collective-permute-done.6
  42.8 0.0 collective-permute-done.7
  42.8 0.0 collective-permute-done.8
  42.9 0.4 collective-permute-done.9
  43.2 0.9 copy-done.9
  44.2 82.4 %shot_gradient.1 = (f32[8,256,128]{2,1,0:T(8,128)}, f32[8,256,128]{2,1,0:T(8,128)}, f32[8,256,128]{2,1,0:T(8,128)}, f32[8,256,128]{2,1,0:T(8,128)}, f32[128,16]{1,0:T(8,128)}) custom-call(s32[32]{0:T(128)} %get-tuple-element.19.take_ref, s32[32]{0:T(128)} %get-tuple-element.18.give_ref, s32[128]{0:T(128)} %copy-done.11, f32[16]{0:T(128)} %wav_ref.1, ...), custom_call_target="tpu_custom_call" | custom-call | tf_op jit(solution)/shard_map/shot_gradient/pallas_call | solution.py:303
  126.6 0.4 collective-permute-start.10
  127.1 0.1 collective-permute-start.14
  127.2 2.4 %collective-permute-done.10 = f32[8,256,128]{2,1,0:T(8,128)S(1)} collective-permute-done((f32[8,256,128]{2,1,0:T(8,128)}, f32[8,256,128]{2,1,0:T(8,128)S(1)}, u32[]{:S(2)}, u32[]{:S(2)}) %collective-permute-start.10) | collective-permute-done | bytes 1048608 | tf_op jit(solution)/shard_map/ppermute | solution.py:350
  129.6 1.5 add.84
  131.1 0.5 collective-permute-start.11
  131.7 0.0 collective-permute-done.14
  131.7 0.1 add.88
  131.8 1.9 %collective-permute-start.15 = (f32[4,256,128]{2,1,0:T(8,128)S(1)}, f32[4,256,128]{2,1,0:T(8,128)S(1)}, u32[]{:S(2)}, u32[]{:S(2)}) collective-permute-start(f32[4,256,128]{2,1,0:T(8,128)S(1)} %slice.65), channel_id=1, source_target_pairs={{0,4},{1,5},{2,6},{3,7},{4,0},{5,1},{6,2},{7,3},{8,12},{9,13},{10,... | collective-permute-start | bytes 1572872 | tf_op jit(solution)/shard_map/ppermute | solution.py:350
  133.7 11.7 %collective-permute-done.11 = f32[4,256,128]{2,1,0:T(8,128)S(1)} collective-permute-done((f32[4,256,128]{2,1,0:T(8,128)S(1)}, f32[4,256,128]{2,1,0:T(8,128)S(1)}, u32[]{:S(2)}, u32[]{:S(2)}) %collective-permute-start.11) | collective-permute-done | bytes 524320 | tf_op jit(solution)/shard_map/ppermute | solution.py:350
  145.4 0.1 slice_add_fusion.1
  145.5 1.8 %collective-permute-start.12 = (f32[2,256,128]{2,1,0:T(8,128)S(1)}, f32[2,256,128]{2,1,0:T(8,128)S(1)}, u32[]{:S(2)}, u32[]{:S(2)}) collective-permute-start(f32[2,256,128]{2,1,0:T(8,128)S(1)} %slice.61), channel_id=1, source_target_pairs={{0,4},{1,5},{2,6},{3,7},{4,0},{5,1},{6,2},{7,3},{8,12},{9,13},{10,... | collective-permute-start | bytes 786440 | tf_op jit(solution)/shard_map/ppermute | solution.py:350
  147.3 0.0 collective-permute-done.15
  147.3 0.1 slice_add_fusion
  147.4 2.6 %collective-permute-start.16 = (f32[2,256,128]{2,1,0:T(8,128)S(1)}, f32[2,256,128]{2,1,0:T(8,128)S(1)}, u32[]{:S(2)}, u32[]{:S(2)}) collective-permute-start(f32[2,256,128]{2,1,0:T(8,128)S(1)} %slice.67), channel_id=1, source_target_pairs={{0,8},{1,9},{2,10},{3,11},{4,12},{5,13},{6,14},{7,15},{8,0},{9,1},... | collective-permute-start | bytes 786440 | tf_op jit(solution)/shard_map/ppermute | solution.py:350
  149.9 0.7 copy.21
  150.6 7.8 %collective-permute-done.12 = f32[2,256,128]{2,1,0:T(8,128)S(1)} collective-permute-done((f32[2,256,128]{2,1,0:T(8,128)S(1)}, f32[2,256,128]{2,1,0:T(8,128)S(1)}, u32[]{:S(2)}, u32[]{:S(2)}) %collective-permute-start.12) | collective-permute-done | bytes 262176 | tf_op jit(solution)/shard_map/ppermute | solution.py:350
  158.4 1.2 collective-permute-start.13
  159.6 5.1 %collective-permute-done.16 = f32[2,256,128]{2,1,0:T(8,128)S(1)} collective-permute-done((f32[2,256,128]{2,1,0:T(8,128)S(1)}, f32[2,256,128]{2,1,0:T(8,128)S(1)}, u32[]{:S(2)}, u32[]{:S(2)}) %collective-permute-start.16) | collective-permute-done | bytes 262176 | tf_op jit(solution)/shard_map/ppermute | solution.py:350
  164.8 0.4 collective-permute-start.17
  165.2 1.9 %collective-permute-done.13 = f32[1,256,128]{2,1,0:T(8,128)S(1)} collective-permute-done((f32[1,256,128]{2,1,0:T(8,128)S(1)}, f32[1,256,128]{2,1,0:T(8,128)S(1)}, u32[]{:S(2)}, u32[]{:S(2)}) %collective-permute-start.13) | collective-permute-done | bytes 131104 | tf_op jit(solution)/shard_map/ppermute | solution.py:350
  167.1 2.7 %collective-permute-done.17 = f32[1,256,128]{2,1,0:T(8,128)S(1)} collective-permute-done((f32[1,256,128]{2,1,0:T(8,128)S(1)}, f32[1,256,128]{2,1,0:T(8,128)S(1)}, u32[]{:S(2)}, u32[]{:S(2)}) %collective-permute-start.17) | collective-permute-done | bytes 131104 | tf_op jit(solution)/shard_map/ppermute | solution.py:350
  169.9 0.7 pad_maximum_fusion.4
  (42 shorter events, 0.4 us)
Async XLA Ops:
  0.6 29.2 %copy-start = (s32[32]{0:T(128)S(1)}, s32[32]{0:T(128)}, u32[]{:S(2)}) copy-start(s32[32]{0:T(128)} %param.15) | copy-start | bytes 388
  1.6 12.5 %collective-permute-start.2 = (f32[1,4,64,128]{3,2,1,0:T(8,128)S(1)}, f32[1,4,64,128]{3,2,1,0:T(8,128)S(1)}, u32[]{:S(2)}, u32[]{:S(2)}) collective-permute-start(f32[1,4,64,128]{3,2,1,0:T(8,128)S(1)} %get-tuple-element.20), channel_id=1, source_target_pairs={{0,2},{1,3},{2,0},{3,1},{4,6},{5,7},{6,4},{7,5},{8,10},{9,11},{10,... | collective-permute-start | bytes 393224 | tf_op jit(solution)/shard_map/ppermute | solution.py:350
  4.7 8.7 %collective-permute-start = (f32[1,4,64,128]{3,2,1,0:T(8,128)S(1)}, f32[1,4,64,128]{3,2,1,0:T(8,128)S(1)}, u32[]{:S(2)}, u32[]{:S(2)}) collective-permute-start(f32[1,4,64,128]{3,2,1,0:T(8,128)S(1)} %get-tuple-element.21), channel_id=1, source_target_pairs={{0,8},{1,9},{2,10},{3,11},{4,12},{5,13},{6,14},{7,15},{8,0},{9,1},... | collective-permute-start | bytes 393224 | tf_op jit(solution)/shard_map/ppermute | solution.py:350
  13.4 12.5 %collective-permute-start.1 = (f32[2,4,64,128]{3,2,1,0:T(8,128)S(1)}, f32[2,4,64,128]{3,2,1,0:T(8,128)S(1)}, u32[]{:S(2)}, u32[]{:S(2)}) collective-permute-start(f32[2,4,64,128]{3,2,1,0:T(8,128)S(1)} %pad_maximum_fusion.2), channel_id=1, source_target_pairs={{0,4},{1,5},{2,6},{3,7},{4,0},{5,1},{6,2},{7,3},{8,12},{9,13},{10,... | collective-permute-start | bytes 786440 | tf_op jit(solution)/shard_map/ppermute | solution.py:350
  14.1 15.3 %collective-permute-start.3 = (f32[2,4,64,128]{3,2,1,0:T(8,128)S(1)}, f32[2,4,64,128]{3,2,1,0:T(8,128)S(1)}, u32[]{:S(2)}, u32[]{:S(2)}) collective-permute-start(f32[2,4,64,128]{3,2,1,0:T(8,128)S(1)} %pad_maximum_fusion.3), channel_id=1, source_target_pairs={{0,8},{1,9},{2,10},{3,11},{4,12},{5,13},{6,14},{7,15},{8,0},{9,1},... | collective-permute-start | bytes 786440 | tf_op jit(solution)/shard_map/ppermute | solution.py:350
  25.9 18.3 %copy-start.1 = (f32[4,4,64,128]{3,2,1,0:T(8,128)}, f32[4,4,64,128]{3,2,1,0:T(8,128)S(1)}, u32[]{:S(2)}) copy-start(f32[4,4,64,128]{3,2,1,0:T(8,128)S(1)} %pad_maximum_fusion) | copy-start | bytes 1572868
  25.9 8.1 %copy-start.16 = (s32[1,16]{1,0:T(1,128)S(1)}, s32[1,16]{1,0:T(1,128)}, u32[]{:S(2)}) copy-start(s32[1,16]{1,0:T(1,128)} %param.16) | copy-start | bytes 196
  26.0 8.1 %copy-start.12 = (s32[32]{0:T(128)S(1)}, s32[32]{0:T(128)}, u32[]{:S(2)}) copy-start(s32[32]{0:T(128)} %constant.74.clone) | copy-start | bytes 388
  26.0 8.1 %copy-start.13 = (s32[32]{0:T(128)S(1)}, s32[32]{0:T(128)}, u32[]{:S(2)}) copy-start(s32[32]{0:T(128)} %constant.73.clone) | copy-start | bytes 388
  26.0 8.1 %copy-start.14 = (s32[32]{0:T(128)S(1)}, s32[32]{0:T(128)}, u32[]{:S(2)}) copy-start(s32[32]{0:T(128)} %constant.72.clone) | copy-start | bytes 388
  26.0 8.1 %copy-start.15 = (s32[32]{0:T(128)S(1)}, s32[32]{0:T(128)}, u32[]{:S(2)}) copy-start(s32[32]{0:T(128)} %constant.71.clone) | copy-start | bytes 388
  26.0 16.0 %copy-start.17 = (s32[1,128]{1,0:T(1,128)S(1)}, s32[1,128]{1,0:T(1,128)}, u32[]{:S(2)}) copy-start(s32[1,128]{1,0:T(1,128)} %param.19) | copy-start | bytes 1540
  26.0 11.5 %collective-permute-start.4 = (f32[4,4,64,128]{3,2,1,0:T(8,128)S(1)}, f32[4,4,64,128]{3,2,1,0:T(8,128)S(1)}, u32[]{:S(2)}, u32[]{:S(2)}) collective-permute-start(f32[4,4,64,128]{3,2,1,0:T(8,128)S(1)} %pad_maximum_fusion), channel_id=1, source_target_pairs={{0,2},{1,3},{2,0},{3,1},{4,6},{5,7},{6,4},{7,5},{8,10},{9,11},{10,... | collective-permute-start | bytes 1572872 | tf_op jit(solution)/shard_map/ppermute | solution.py:350
  29.5 14.7 %copy-start.2 = (f32[4,4,64,128]{3,2,1,0:T(8,128)}, f32[4,4,64,128]{3,2,1,0:T(8,128)S(1)}, u32[]{:S(2)}) copy-start(f32[4,4,64,128]{3,2,1,0:T(8,128)S(1)} %pad_maximum_fusion.1) | copy-start | bytes 1572868
  29.5 11.8 %collective-permute-start.5 = (f32[4,4,64,128]{3,2,1,0:T(8,128)S(1)}, f32[4,4,64,128]{3,2,1,0:T(8,128)S(1)}, u32[]{:S(2)}, u32[]{:S(2)}) collective-permute-start(f32[4,4,64,128]{3,2,1,0:T(8,128)S(1)} %pad_maximum_fusion.1), channel_id=1, source_target_pairs={{0,4},{1,5},{2,6},{3,7},{4,0},{5,1},{6,2},{7,3},{8,12},{9,13},{10,... | collective-permute-start | bytes 1572872 | tf_op jit(solution)/shard_map/ppermute | solution.py:350
  34.1 8.7 %collective-permute-start.6 = (f32[4,4,64,128]{3,2,1,0:T(8,128)S(1)}, f32[4,4,64,128]{3,2,1,0:T(8,128)S(1)}, u32[]{:S(2)}, u32[]{:S(2)}) collective-permute-start(f32[4,4,64,128]{3,2,1,0:T(8,128)S(1)} %pad_maximum_fusion), channel_id=1, source_target_pairs={{0,1},{1,0},{2,3},{3,2},{4,5},{5,4},{6,7},{7,6},{8,9},{9,8},{10,11... | collective-permute-start | bytes 1572872 | tf_op jit(solution)/shard_map/ppermute | solution.py:350
  34.2 8.7 %collective-permute-start.7 = (f32[4,4,64,128]{3,2,1,0:T(8,128)S(1)}, f32[4,4,64,128]{3,2,1,0:T(8,128)S(1)}, u32[]{:S(2)}, u32[]{:S(2)}) collective-permute-start(f32[4,4,64,128]{3,2,1,0:T(8,128)S(1)} %pad_maximum_fusion.1), channel_id=1, source_target_pairs={{0,1},{1,0},{2,3},{3,2},{4,5},{5,4},{6,7},{7,6},{8,9},{9,8},{10,11... | collective-permute-start | bytes 1572872 | tf_op jit(solution)/shard_map/ppermute | solution.py:350
  37.5 6.7 %copy-start.4 = (f32[4,4,64,128]{3,2,1,0:T(8,128)}, f32[4,4,64,128]{3,2,1,0:T(8,128)S(1)}, u32[]{:S(2)}) copy-start(f32[4,4,64,128]{3,2,1,0:T(8,128)S(1)} %collective-permute-done.4) | copy-start | bytes 1572868
  37.5 5.3 %collective-permute-start.8 = (f32[4,4,64,128]{3,2,1,0:T(8,128)S(1)}, f32[4,4,64,128]{3,2,1,0:T(8,128)S(1)}, u32[]{:S(2)}, u32[]{:S(2)}) collective-permute-start(f32[4,4,64,128]{3,2,1,0:T(8,128)S(1)} %collective-permute-done.4), channel_id=1, source_target_pairs={{0,1},{1,0},{2,3},{3,2},{4,5},{5,4},{6,7},{7,6},{8,9},{9,8},{10,11... | collective-permute-start | bytes 1572872 | tf_op jit(solution)/shard_map/ppermute | solution.py:350
  41.3 2.9 %copy-start.5 = (f32[4,4,64,128]{3,2,1,0:T(8,128)}, f32[4,4,64,128]{3,2,1,0:T(8,128)S(1)}, u32[]{:S(2)}) copy-start(f32[4,4,64,128]{3,2,1,0:T(8,128)S(1)} %collective-permute-done.5) | copy-start | bytes 1572868
  41.3 1.9 %collective-permute-start.9 = (f32[4,4,64,128]{3,2,1,0:T(8,128)S(1)}, f32[4,4,64,128]{3,2,1,0:T(8,128)S(1)}, u32[]{:S(2)}, u32[]{:S(2)}) collective-permute-start(f32[4,4,64,128]{3,2,1,0:T(8,128)S(1)} %collective-permute-done.5), channel_id=1, source_target_pairs={{0,1},{1,0},{2,3},{3,2},{4,5},{5,4},{6,7},{7,6},{8,9},{9,8},{10,11... | collective-permute-start | bytes 1572872 | tf_op jit(solution)/shard_map/ppermute | solution.py:350
  42.1 2.1 %copy-start.11 = (s32[128]{0:T(128)}, s32[128]{0:T(128)S(1)}, u32[]{:S(2)}) copy-start(s32[128]{0:T(128)S(1)} %get-tuple-element.23.rec_ref) | copy-start | bytes 1540
  42.8 1.4 copy-start.6
  42.8 1.4 copy-start.7
  42.9 1.4 copy-start.8
  43.2 0.9 copy-start.9
  126.6 2.9 %collective-permute-start.10 = (f32[8,256,128]{2,1,0:T(8,128)}, f32[8,256,128]{2,1,0:T(8,128)S(1)}, u32[]{:S(2)}, u32[]{:S(2)}) collective-permute-start(f32[8,256,128]{2,1,0:T(8,128)} %get-tuple-element.8), channel_id=1, source_target_pairs={{0,1},{1,0},{2,3},{3,2},{4,5},{5,4},{6,7},{7,6},{8,9},{9,8},{10,11... | collective-permute-start | bytes 3145736 | tf_op jit(solution)/shard_map/ppermute | solution.py:350
  127.1 4.6 %collective-permute-start.14 = (f32[8,256,128]{2,1,0:T(8,128)}, f32[8,256,128]{2,1,0:T(8,128)S(1)}, u32[]{:S(2)}, u32[]{:S(2)}) collective-permute-start(f32[8,256,128]{2,1,0:T(8,128)} %get-tuple-element.10), channel_id=1, source_target_pairs={{0,1},{1,0},{2,3},{3,2},{4,5},{5,4},{6,7},{7,6},{8,9},{9,8},{10,11... | collective-permute-start | bytes 3145736 | tf_op jit(solution)/shard_map/ppermute | solution.py:350
  129.6 2.1 %copy-start.3 = (f32[8,256,128]{2,1,0:T(8,128)S(1)}, f32[8,256,128]{2,1,0:T(8,128)}, u32[]{:S(2)}) copy-start(f32[8,256,128]{2,1,0:T(8,128)} %get-tuple-element.9) | copy-start | bytes 3145732
  131.1 14.3 %collective-permute-start.11 = (f32[4,256,128]{2,1,0:T(8,128)S(1)}, f32[4,256,128]{2,1,0:T(8,128)S(1)}, u32[]{:S(2)}, u32[]{:S(2)}) collective-permute-start(f32[4,256,128]{2,1,0:T(8,128)S(1)} %slice.59), channel_id=1, source_target_pairs={{0,2},{1,3},{2,0},{3,1},{4,6},{5,7},{6,4},{7,5},{8,10},{9,11},{10,... | collective-permute-start | bytes 1572872 | tf_op jit(solution)/shard_map/ppermute | solution.py:350
  131.8 18.1 %copy-start.10 = (f32[128,16]{1,0:T(8,128)S(1)}, f32[128,16]{1,0:T(8,128)}, u32[]{:S(2)}) copy-start(f32[128,16]{1,0:T(8,128)} %get-tuple-element.11) | copy-start | bytes 24580
  131.8 15.4 %collective-permute-start.15 = (f32[4,256,128]{2,1,0:T(8,128)S(1)}, f32[4,256,128]{2,1,0:T(8,128)S(1)}, u32[]{:S(2)}, u32[]{:S(2)}) collective-permute-start(f32[4,256,128]{2,1,0:T(8,128)S(1)} %slice.65), channel_id=1, source_target_pairs={{0,4},{1,5},{2,6},{3,7},{4,0},{5,1},{6,2},{7,3},{8,12},{9,13},{10,... | collective-permute-start | bytes 1572872 | tf_op jit(solution)/shard_map/ppermute | solution.py:350
  145.5 12.9 %collective-permute-start.12 = (f32[2,256,128]{2,1,0:T(8,128)S(1)}, f32[2,256,128]{2,1,0:T(8,128)S(1)}, u32[]{:S(2)}, u32[]{:S(2)}) collective-permute-start(f32[2,256,128]{2,1,0:T(8,128)S(1)} %slice.61), channel_id=1, source_target_pairs={{0,4},{1,5},{2,6},{3,7},{4,0},{5,1},{6,2},{7,3},{8,12},{9,13},{10,... | collective-permute-start | bytes 786440 | tf_op jit(solution)/shard_map/ppermute | solution.py:350
  147.4 17.4 %collective-permute-start.16 = (f32[2,256,128]{2,1,0:T(8,128)S(1)}, f32[2,256,128]{2,1,0:T(8,128)S(1)}, u32[]{:S(2)}, u32[]{:S(2)}) collective-permute-start(f32[2,256,128]{2,1,0:T(8,128)S(1)} %slice.67), channel_id=1, source_target_pairs={{0,8},{1,9},{2,10},{3,11},{4,12},{5,13},{6,14},{7,15},{8,0},{9,1},... | collective-permute-start | bytes 786440 | tf_op jit(solution)/shard_map/ppermute | solution.py:350
  158.4 8.7 %collective-permute-start.13 = (f32[1,256,128]{2,1,0:T(8,128)S(1)}, f32[1,256,128]{2,1,0:T(8,128)S(1)}, u32[]{:S(2)}, u32[]{:S(2)}) collective-permute-start(f32[1,256,128]{2,1,0:T(8,128)S(1)} %slice.63), channel_id=1, source_target_pairs={{0,8},{1,9},{2,10},{3,11},{4,12},{5,13},{6,14},{7,15},{8,0},{9,1},... | collective-permute-start | bytes 393224 | tf_op jit(solution)/shard_map/ppermute | solution.py:350
  164.8 5.0 %collective-permute-start.17 = (f32[1,256,128]{2,1,0:T(8,128)S(1)}, f32[1,256,128]{2,1,0:T(8,128)S(1)}, u32[]{:S(2)}, u32[]{:S(2)}) collective-permute-start(f32[1,256,128]{2,1,0:T(8,128)S(1)} %slice.69), channel_id=1, source_target_pairs={{0,2},{1,3},{2,0},{3,1},{4,6},{5,7},{6,4},{7,5},{8,10},{9,11},{10,... | collective-permute-start | bytes 393224 | tf_op jit(solution)/shard_map/ppermute | solution.py:350

commit v4 on v3

--- a/solution.py
+++ b/solution.py
@@ -15,7 +15,7 @@
 SCALE = 128.0 / 5040.0
 REACH = 4
 LANES = 128
-GROUP = 8
+GROUP = 16
 
 
 def band(size, center):
@@ -121,17 +121,19 @@
 
     def combine(base, of, taps, update):
         for j in range(0, ny, 16):
-            near = [fields[of][pl.ds(base + d * ny + j, 16), :] for d in range(GROUP + 2 * REACH)]
-            for i in range(GROUP):
-                lap = near[i + 4 - 3] + near[i + 4 + 3]
-                lap = lap + TAPS[0] * (near[i + 4 - 1] + near[i + 4 + 1])
-                lap = lap + TAPS[1] * (near[i + 4 - 2] + near[i + 4 + 2])
-                lap = lap + TAPS[3] * (near[i + 4 - 4] + near[i + 4 + 4])
-                lap = lap + taps[i * ny + j : i * ny + j + 16, :]
-                at = base + i * ny + j
-                update(at if isinstance(at, int) else pl.multiple_of(at, 16), near[i + 4], lap)
-
-    def sweep(of, update):
+            for h in range(0, GROUP, 4):
+                near = [fields[of][pl.ds(base + (h + d) * ny + j, 16), :] for d in range(4 + 2 * REACH)]
+                for i in range(4):
+                    lap = near[i + 4 - 3] + near[i + 4 + 3]
+                    lap = lap + TAPS[0] * (near[i + 4 - 1] + near[i + 4 + 1])
+                    lap = lap + TAPS[1] * (near[i + 4 - 2] + near[i + 4 + 2])
+                    lap = lap + TAPS[3] * (near[i + 4 - 4] + near[i + 4 + 4])
+                    at = (h + i) * ny + j
+                    lap = lap + taps[at : at + 16, :]
+                    at = base + at
+                    update(at if isinstance(at, int) else pl.multiple_of(at, 16), near[i + 4], lap)
+
+    def sweep(of, update, ahead=True):
         def body(g, _):
             base = pl.multiple_of(g * (2 * block), 2 * block)
             multiply(base + block, of, taps_b)
@@ -144,7 +146,8 @@
         base = (groups - 2) * block
         multiply(base + block, of, taps_b)
         combine(base, of, taps_a, update)
-        multiply(0, 1 - of, taps_a)
+        if ahead:
+            multiply(0, 1 - of, taps_a)
         combine(base + block, of, taps_b, update)
 
     def rows16(fn):
@@ -175,7 +178,7 @@
 
     rows16(squared)
 
-    def forward(n, of):
+    def forward(n, of, ahead=True):
         strength = wav_ref[n]
 
         def update(at, here, lap):
@@ -185,9 +188,10 @@
             value = here + here_rate
             hist[1 - of][n // 2, pl.ds(at, 16), :] = here_rate
             fields[1 - of][pl.ds(edge + at, 16), :] = value
-            keep(1 - of, at, value)
-
-        sweep(of, update)
+            if ahead:
+                keep(1 - of, at, value)
+
+        sweep(of, update, ahead)
         listen(n, 1 - of)
 
     def forward_pair(k, _):
@@ -197,7 +201,7 @@
 
     lax.fori_loop(0, (nstep - 1) // 2, forward_pair, 0)
     if nstep % 2 == 0:
-        forward(nstep - 1, 0)
+        forward(nstep - 1, 0, False)
 
     step_lane = lax.broadcasted_iota(jnp.int32, (nrec, nstep), 1)
 
@@ -272,11 +276,11 @@
         image = dense[pl.ds(at, 16), :] - hist_a[0, pl.ds(at, 16), :] * end[pl.ds(edge + at, 16), :]
         dense[pl.ds(at, 16), :] = (2.0 / region[pl.ds(at, 16), :]) * image
 
-    rows16(finish)
-
     for r in range(held):
         @pl.when(give_ref[r] >= 0)
         def _():
+            for j in range(0, slab, 16):
+                finish(pl.multiple_of(give_ref[r] * slab + j, 16))
             give(r).start()
 
     for r in range(held):

time: 171 us -> 168 us (0.982)
  Pallas kernels: 82.4 us -> 79.4 us
    pallas_call x1, Pallas kernels: 82.4 us -> 79.4 us  [shot(): pl.pallas_call(functools.partial(kernel, len(pieces), targets), out_shape...]
where the time goes in v4:
time: 168 us
  Pallas kernels  79.4 us (47%)
  waiting for transfers between devices  52.3 us (31%)
  starting transfers between devices  20.3 us (12%)
  other arithmetic  9.7 us (6%)
  local copies, waits for them, and re-layouts  4.91 us (3%)
    pallas_call x1, Pallas kernels, shot(): pl.pallas_call(functools.partial(kernel, len(pieces), targets), out_shape...  79.4 us
    ppermute x18, waiting for transfers between devices, trade(): lax.ppermute(block, 'shot', [(i, i ^ flip) for i in range(SIDE_Z * SIDE_Y...  52.3 us
    ppermute x18, starting transfers between devices, trade(): lax.ppermute(block, 'shot', [(i, i ^ flip) for i in range(SIDE_Z * SIDE_Y...  20.3 us
    scatter-add x1, other arithmetic, shards(): jnp.zeros((cells * nz,), jnp.float32).at[source_at[0]].add(source_amp[0])  3.55 us
  transfers between devices with their start and end apart: 18, of which 12 were waited for; matrix products, arithmetic and copies ran while one was open for 7% of the time, Pallas kernels for 0%

profile of v4, /device:TPU:0, one launch (start us, length us, event | category | flops | bytes accessed | tf_op | source)
XLA Modules:
  0.0 167.6 jit_solution(3088007633163586544)
XLA Ops:
  0.6 0.0 copy-start
  0.6 1.0 fusion.6
  1.6 3.0 %collective-permute-start.2 = (f32[1,4,64,128]{3,2,1,0:T(8,128)S(1)}, f32[1,4,64,128]{3,2,1,0:T(8,128)S(1)}, u32[]{:S(2)}, u32[]{:S(2)}) collective-permute-start(f32[1,4,64,128]{3,2,1,0:T(8,128)S(1)} %get-tuple-element.20), channel_id=1, source_target_pairs={{0,2},{1,3},{2,0},{3,1},{4,6},{5,7},{6,4},{7,5},{8,10},{9,11},{10,... | collective-permute-start | bytes 393224 | tf_op jit(solution)/shard_map/ppermute | solution.py:354
  4.7 2.6 %collective-permute-start = (f32[1,4,64,128]{3,2,1,0:T(8,128)S(1)}, f32[1,4,64,128]{3,2,1,0:T(8,128)S(1)}, u32[]{:S(2)}, u32[]{:S(2)}) collective-permute-start(f32[1,4,64,128]{3,2,1,0:T(8,128)S(1)} %get-tuple-element.21), channel_id=1, source_target_pairs={{0,8},{1,9},{2,10},{3,11},{4,12},{5,13},{6,14},{7,15},{8,0},{9,1},... | collective-permute-start | bytes 393224 | tf_op jit(solution)/shard_map/ppermute | solution.py:354
  7.3 0.7 compare_select_fusion
  7.9 0.7 fusion.3
  8.6 1.4 copy.20
  10.0 3.3 %collective-permute-done = f32[1,4,64,128]{3,2,1,0:T(8,128)S(1)} collective-permute-done((f32[1,4,64,128]{3,2,1,0:T(8,128)S(1)}, f32[1,4,64,128]{3,2,1,0:T(8,128)S(1)}, u32[]{:S(2)}, u32[]{:S(2)}) %collective-permute-start) | collective-permute-done | bytes 131104 | tf_op jit(solution)/shard_map/ppermute | solution.py:354
  13.4 0.7 collective-permute-start.1
  14.1 0.0 collective-permute-done.2
  14.1 3.4 %collective-permute-start.3 = (f32[2,4,64,128]{3,2,1,0:T(8,128)S(1)}, f32[2,4,64,128]{3,2,1,0:T(8,128)S(1)}, u32[]{:S(2)}, u32[]{:S(2)}) collective-permute-start(f32[2,4,64,128]{3,2,1,0:T(8,128)S(1)} %pad_maximum_fusion.3), channel_id=1, source_target_pairs={{0,8},{1,9},{2,10},{3,11},{4,12},{5,13},{6,14},{7,15},{8,0},{9,1},... | collective-permute-start | bytes 786440 | tf_op jit(solution)/shard_map/ppermute | solution.py:354
  17.6 0.7 fusion.5
  18.2 7.7 %collective-permute-done.1 = f32[2,4,64,128]{3,2,1,0:T(8,128)S(1)} collective-permute-done((f32[2,4,64,128]{3,2,1,0:T(8,128)S(1)}, f32[2,4,64,128]{3,2,1,0:T(8,128)S(1)}, u32[]{:S(2)}, u32[]{:S(2)}) %collective-permute-start.1) | collective-permute-done | bytes 262176 | tf_op jit(solution)/shard_map/ppermute | solution.py:354
  25.9 0.0 copy-start.1
  25.9 0.0 copy-start.16
  26.0 0.0 copy-start.12
  26.0 0.0 copy-start.13
  26.0 0.0 copy-start.14
  26.0 0.0 copy-start.15
  26.0 0.0 copy-start.17
  26.0 0.6 collective-permute-start.4
  26.6 2.8 %collective-permute-done.3 = f32[2,4,64,128]{3,2,1,0:T(8,128)S(1)} collective-permute-done((f32[2,4,64,128]{3,2,1,0:T(8,128)S(1)}, f32[2,4,64,128]{3,2,1,0:T(8,128)S(1)}, u32[]{:S(2)}, u32[]{:S(2)}) %collective-permute-start.3) | collective-permute-done | bytes 262176 | tf_op jit(solution)/shard_map/ppermute | solution.py:354
  29.5 0.3 collective-permute-start.5
  29.8 0.0 copy-done
  29.8 0.7 gather_fusion
  30.5 3.6 %scatter_custom_fusion = f32[524288]{0:T(1024)} fusion(s32[256]{0:T(256)S(1)} %bitcast.59, f32[256]{0:T(256)} %bitcast.60, f32[]{:T(128)} %constant.68.clone.1), kind=kCustom, calls=%fused_computation.2 | custom fusion | flops 256 | bytes 2097664 | tf_op jit(solution)/shard_map/scatter-add | solution.py:422
  34.1 0.1 collective-permute-start.6
  34.2 0.5 collective-permute-start.7
  34.7 2.8 %collective-permute-done.4 = f32[4,4,64,128]{3,2,1,0:T(8,128)S(1)} collective-permute-done((f32[4,4,64,128]{3,2,1,0:T(8,128)S(1)}, f32[4,4,64,128]{3,2,1,0:T(8,128)S(1)}, u32[]{:S(2)}, u32[]{:S(2)}) %collective-permute-start.4) | collective-permute-done | bytes 524320 | tf_op jit(solution)/shard_map/ppermute | solution.py:354
  37.5 0.0 collective-permute-start.8
  37.5 3.8 %collective-permute-done.5 = f32[4,4,64,128]{3,2,1,0:T(8,128)S(1)} collective-permute-done((f32[4,4,64,128]{3,2,1,0:T(8,128)S(1)}, f32[4,4,64,128]{3,2,1,0:T(8,128)S(1)}, u32[]{:S(2)}, u32[]{:S(2)}) %collective-permute-start.5) | collective-permute-done | bytes 524320 | tf_op jit(solution)/shard_map/ppermute | solution.py:354
  41.3 0.0 collective-permute-start.9
  41.3 0.7 select_reduce_fusion
  42.0 0.0 copy-done.17
  42.1 0.8 fusion.2
  42.8 0.0 collective-permute-done.6
  42.8 0.0 collective-permute-done.7
  42.8 0.0 collective-permute-done.8
  42.9 0.4 collective-permute-done.9
  43.2 0.9 copy-done.9
  44.2 0.0 copy-done.1
  44.2 79.4 %shot_gradient.1 = (f32[8,256,128]{2,1,0:T(8,128)}, f32[8,256,128]{2,1,0:T(8,128)}, f32[8,256,128]{2,1,0:T(8,128)}, f32[8,256,128]{2,1,0:T(8,128)}, f32[128,16]{1,0:T(8,128)}) custom-call(s32[32]{0:T(128)} %get-tuple-element.19.take_ref, s32[32]{0:T(128)} %get-tuple-element.18.give_ref, s32[128]{0:T(128)} %copy-done.11, f32[16]{0:T(128)} %wav_ref.1, ...), custom_call_target="tpu_custom_call" | custom-call | tf_op jit(solution)/shard_map/shot_gradient/pallas_call | solution.py:307
  123.7 0.4 collective-permute-start.10
  124.1 0.1 collective-permute-start.14
  124.2 2.4 %collective-permute-done.10 = f32[8,256,128]{2,1,0:T(8,128)S(1)} collective-permute-done((f32[8,256,128]{2,1,0:T(8,128)}, f32[8,256,128]{2,1,0:T(8,128)S(1)}, u32[]{:S(2)}, u32[]{:S(2)}) %collective-permute-start.10) | collective-permute-done | bytes 1048608 | tf_op jit(solution)/shard_map/ppermute | solution.py:354
  126.6 1.5 add.84
  128.2 0.6 collective-permute-start.11
  128.8 0.0 collective-permute-done.14
  128.8 0.1 add.88
  128.9 1.8 %collective-permute-start.15 = (f32[4,256,128]{2,1,0:T(8,128)S(1)}, f32[4,256,128]{2,1,0:T(8,128)S(1)}, u32[]{:S(2)}, u32[]{:S(2)}) collective-permute-start(f32[4,256,128]{2,1,0:T(8,128)S(1)} %slice.65), channel_id=1, source_target_pairs={{0,4},{1,5},{2,6},{3,7},{4,0},{5,1},{6,2},{7,3},{8,12},{9,13},{10,... | collective-permute-start | bytes 1572872 | tf_op jit(solution)/shard_map/ppermute | solution.py:354
  130.7 11.7 %collective-permute-done.11 = f32[4,256,128]{2,1,0:T(8,128)S(1)} collective-permute-done((f32[4,256,128]{2,1,0:T(8,128)S(1)}, f32[4,256,128]{2,1,0:T(8,128)S(1)}, u32[]{:S(2)}, u32[]{:S(2)}) %collective-permute-start.11) | collective-permute-done | bytes 524320 | tf_op jit(solution)/shard_map/ppermute | solution.py:354
  142.4 0.1 slice_add_fusion.1
  142.5 1.8 %collective-permute-start.12 = (f32[2,256,128]{2,1,0:T(8,128)S(1)}, f32[2,256,128]{2,1,0:T(8,128)S(1)}, u32[]{:S(2)}, u32[]{:S(2)}) collective-permute-start(f32[2,256,128]{2,1,0:T(8,128)S(1)} %slice.61), channel_id=1, source_target_pairs={{0,4},{1,5},{2,6},{3,7},{4,0},{5,1},{6,2},{7,3},{8,12},{9,13},{10,... | collective-permute-start | bytes 786440 | tf_op jit(solution)/shard_map/ppermute | solution.py:354
  144.3 0.0 collective-permute-done.15
  144.3 0.1 slice_add_fusion
  144.4 2.5 %collective-permute-start.16 = (f32[2,256,128]{2,1,0:T(8,128)S(1)}, f32[2,256,128]{2,1,0:T(8,128)S(1)}, u32[]{:S(2)}, u32[]{:S(2)}) collective-permute-start(f32[2,256,128]{2,1,0:T(8,128)S(1)} %slice.67), channel_id=1, source_target_pairs={{0,8},{1,9},{2,10},{3,11},{4,12},{5,13},{6,14},{7,15},{8,0},{9,1},... | collective-permute-start | bytes 786440 | tf_op jit(solution)/shard_map/ppermute | solution.py:354
  146.9 0.7 copy.21
  147.6 7.8 %collective-permute-done.12 = f32[2,256,128]{2,1,0:T(8,128)S(1)} collective-permute-done((f32[2,256,128]{2,1,0:T(8,128)S(1)}, f32[2,256,128]{2,1,0:T(8,128)S(1)}, u32[]{:S(2)}, u32[]{:S(2)}) %collective-permute-start.12) | collective-permute-done | bytes 262176 | tf_op jit(solution)/shard_map/ppermute | solution.py:354
  155.4 1.2 collective-permute-start.13
  156.6 5.2 %collective-permute-done.16 = f32[2,256,128]{2,1,0:T(8,128)S(1)} collective-permute-done((f32[2,256,128]{2,1,0:T(8,128)S(1)}, f32[2,256,128]{2,1,0:T(8,128)S(1)}, u32[]{:S(2)}, u32[]{:S(2)}) %collective-permute-start.16) | collective-permute-done | bytes 262176 | tf_op jit(solution)/shard_map/ppermute | solution.py:354
  161.8 0.6 collective-permute-start.17
  162.4 1.7 collective-permute-done.13
  164.1 2.8 %collective-permute-done.17 = f32[1,256,128]{2,1,0:T(8,128)S(1)} collective-permute-done((f32[1,256,128]{2,1,0:T(8,128)S(1)}, f32[1,256,128]{2,1,0:T(8,128)S(1)}, u32[]{:S(2)}, u32[]{:S(2)}) %collective-permute-start.17) | collective-permute-done | bytes 131104 | tf_op jit(solution)/shard_map/ppermute | solution.py:354
  166.9 0.7 pad_maximum_fusion.4
  (42 shorter events, 0.4 us)
Async XLA Ops:
  0.6 29.2 %copy-start = (s32[32]{0:T(128)S(1)}, s32[32]{0:T(128)}, u32[]{:S(2)}) copy-start(s32[32]{0:T(128)} %param.15) | copy-start | bytes 388
  1.6 12.5 %collective-permute-start.2 = (f32[1,4,64,128]{3,2,1,0:T(8,128)S(1)}, f32[1,4,64,128]{3,2,1,0:T(8,128)S(1)}, u32[]{:S(2)}, u32[]{:S(2)}) collective-permute-start(f32[1,4,64,128]{3,2,1,0:T(8,128)S(1)} %get-tuple-element.20), channel_id=1, source_target_pairs={{0,2},{1,3},{2,0},{3,1},{4,6},{5,7},{6,4},{7,5},{8,10},{9,11},{10,... | collective-permute-start | bytes 393224 | tf_op jit(solution)/shard_map/ppermute | solution.py:354
  4.7 8.7 %collective-permute-start = (f32[1,4,64,128]{3,2,1,0:T(8,128)S(1)}, f32[1,4,64,128]{3,2,1,0:T(8,128)S(1)}, u32[]{:S(2)}, u32[]{:S(2)}) collective-permute-start(f32[1,4,64,128]{3,2,1,0:T(8,128)S(1)} %get-tuple-element.21), channel_id=1, source_target_pairs={{0,8},{1,9},{2,10},{3,11},{4,12},{5,13},{6,14},{7,15},{8,0},{9,1},... | collective-permute-start | bytes 393224 | tf_op jit(solution)/shard_map/ppermute | solution.py:354
  13.4 12.5 %collective-permute-start.1 = (f32[2,4,64,128]{3,2,1,0:T(8,128)S(1)}, f32[2,4,64,128]{3,2,1,0:T(8,128)S(1)}, u32[]{:S(2)}, u32[]{:S(2)}) collective-permute-start(f32[2,4,64,128]{3,2,1,0:T(8,128)S(1)} %pad_maximum_fusion.2), channel_id=1, source_target_pairs={{0,4},{1,5},{2,6},{3,7},{4,0},{5,1},{6,2},{7,3},{8,12},{9,13},{10,... | collective-permute-start | bytes 786440 | tf_op jit(solution)/shard_map/ppermute | solution.py:354
  14.1 15.3 %collective-permute-start.3 = (f32[2,4,64,128]{3,2,1,0:T(8,128)S(1)}, f32[2,4,64,128]{3,2,1,0:T(8,128)S(1)}, u32[]{:S(2)}, u32[]{:S(2)}) collective-permute-start(f32[2,4,64,128]{3,2,1,0:T(8,128)S(1)} %pad_maximum_fusion.3), channel_id=1, source_target_pairs={{0,8},{1,9},{2,10},{3,11},{4,12},{5,13},{6,14},{7,15},{8,0},{9,1},... | collective-permute-start | bytes 786440 | tf_op jit(solution)/shard_map/ppermute | solution.py:354
  25.9 18.3 %copy-start.1 = (f32[4,4,64,128]{3,2,1,0:T(8,128)}, f32[4,4,64,128]{3,2,1,0:T(8,128)S(1)}, u32[]{:S(2)}) copy-start(f32[4,4,64,128]{3,2,1,0:T(8,128)S(1)} %pad_maximum_fusion) | copy-start | bytes 1572868
  25.9 8.1 %copy-start.16 = (s32[1,16]{1,0:T(1,128)S(1)}, s32[1,16]{1,0:T(1,128)}, u32[]{:S(2)}) copy-start(s32[1,16]{1,0:T(1,128)} %param.16) | copy-start | bytes 196
  26.0 8.1 %copy-start.12 = (s32[32]{0:T(128)S(1)}, s32[32]{0:T(128)}, u32[]{:S(2)}) copy-start(s32[32]{0:T(128)} %constant.74.clone) | copy-start | bytes 388
  26.0 8.1 %copy-start.13 = (s32[32]{0:T(128)S(1)}, s32[32]{0:T(128)}, u32[]{:S(2)}) copy-start(s32[32]{0:T(128)} %constant.73.clone) | copy-start | bytes 388
  26.0 8.1 %copy-start.14 = (s32[32]{0:T(128)S(1)}, s32[32]{0:T(128)}, u32[]{:S(2)}) copy-start(s32[32]{0:T(128)} %constant.72.clone) | copy-start | bytes 388
  26.0 8.1 %copy-start.15 = (s32[32]{0:T(128)S(1)}, s32[32]{0:T(128)}, u32[]{:S(2)}) copy-start(s32[32]{0:T(128)} %constant.71.clone) | copy-start | bytes 388
  26.0 16.0 %copy-start.17 = (s32[1,128]{1,0:T(1,128)S(1)}, s32[1,128]{1,0:T(1,128)}, u32[]{:S(2)}) copy-start(s32[1,128]{1,0:T(1,128)} %param.19) | copy-start | bytes 1540
  26.0 11.5 %collective-permute-start.4 = (f32[4,4,64,128]{3,2,1,0:T(8,128)S(1)}, f32[4,4,64,128]{3,2,1,0:T(8,128)S(1)}, u32[]{:S(2)}, u32[]{:S(2)}) collective-permute-start(f32[4,4,64,128]{3,2,1,0:T(8,128)S(1)} %pad_maximum_fusion), channel_id=1, source_target_pairs={{0,2},{1,3},{2,0},{3,1},{4,6},{5,7},{6,4},{7,5},{8,10},{9,11},{10,... | collective-permute-start | bytes 1572872 | tf_op jit(solution)/shard_map/ppermute | solution.py:354
  29.5 14.7 %copy-start.2 = (f32[4,4,64,128]{3,2,1,0:T(8,128)}, f32[4,4,64,128]{3,2,1,0:T(8,128)S(1)}, u32[]{:S(2)}) copy-start(f32[4,4,64,128]{3,2,1,0:T(8,128)S(1)} %pad_maximum_fusion.1) | copy-start | bytes 1572868
  29.5 11.8 %collective-permute-start.5 = (f32[4,4,64,128]{3,2,1,0:T(8,128)S(1)}, f32[4,4,64,128]{3,2,1,0:T(8,128)S(1)}, u32[]{:S(2)}, u32[]{:S(2)}) collective-permute-start(f32[4,4,64,128]{3,2,1,0:T(8,128)S(1)} %pad_maximum_fusion.1), channel_id=1, source_target_pairs={{0,4},{1,5},{2,6},{3,7},{4,0},{5,1},{6,2},{7,3},{8,12},{9,13},{10,... | collective-permute-start | bytes 1572872 | tf_op jit(solution)/shard_map/ppermute | solution.py:354
  34.1 8.7 %collective-permute-start.6 = (f32[4,4,64,128]{3,2,1,0:T(8,128)S(1)}, f32[4,4,64,128]{3,2,1,0:T(8,128)S(1)}, u32[]{:S(2)}, u32[]{:S(2)}) collective-permute-start(f32[4,4,64,128]{3,2,1,0:T(8,128)S(1)} %pad_maximum_fusion), channel_id=1, source_target_pairs={{0,1},{1,0},{2,3},{3,2},{4,5},{5,4},{6,7},{7,6},{8,9},{9,8},{10,11... | collective-permute-start | bytes 1572872 | tf_op jit(solution)/shard_map/ppermute | solution.py:354
  34.2 8.7 %collective-permute-start.7 = (f32[4,4,64,128]{3,2,1,0:T(8,128)S(1)}, f32[4,4,64,128]{3,2,1,0:T(8,128)S(1)}, u32[]{:S(2)}, u32[]{:S(2)}) collective-permute-start(f32[4,4,64,128]{3,2,1,0:T(8,128)S(1)} %pad_maximum_fusion.1), channel_id=1, source_target_pairs={{0,1},{1,0},{2,3},{3,2},{4,5},{5,4},{6,7},{7,6},{8,9},{9,8},{10,11... | collective-permute-start | bytes 1572872 | tf_op jit(solution)/shard_map/ppermute | solution.py:354
  37.5 6.7 %copy-start.4 = (f32[4,4,64,128]{3,2,1,0:T(8,128)}, f32[4,4,64,128]{3,2,1,0:T(8,128)S(1)}, u32[]{:S(2)}) copy-start(f32[4,4,64,128]{3,2,1,0:T(8,128)S(1)} %collective-permute-done.4) | copy-start | bytes 1572868
  37.5 5.3 %collective-permute-start.8 = (f32[4,4,64,128]{3,2,1,0:T(8,128)S(1)}, f32[4,4,64,128]{3,2,1,0:T(8,128)S(1)}, u32[]{:S(2)}, u32[]{:S(2)}) collective-permute-start(f32[4,4,64,128]{3,2,1,0:T(8,128)S(1)} %collective-permute-done.4), channel_id=1, source_target_pairs={{0,1},{1,0},{2,3},{3,2},{4,5},{5,4},{6,7},{7,6},{8,9},{9,8},{10,11... | collective-permute-start | bytes 1572872 | tf_op jit(solution)/shard_map/ppermute | solution.py:354
  41.3 2.9 %copy-start.5 = (f32[4,4,64,128]{3,2,1,0:T(8,128)}, f32[4,4,64,128]{3,2,1,0:T(8,128)S(1)}, u32[]{:S(2)}) copy-start(f32[4,4,64,128]{3,2,1,0:T(8,128)S(1)} %collective-permute-done.5) | copy-start | bytes 1572868
  41.3 1.9 %collective-permute-start.9 = (f32[4,4,64,128]{3,2,1,0:T(8,128)S(1)}, f32[4,4,64,128]{3,2,1,0:T(8,128)S(1)}, u32[]{:S(2)}, u32[]{:S(2)}) collective-permute-start(f32[4,4,64,128]{3,2,1,0:T(8,128)S(1)} %collective-permute-done.5), channel_id=1, source_target_pairs={{0,1},{1,0},{2,3},{3,2},{4,5},{5,4},{6,7},{7,6},{8,9},{9,8},{10,11... | collective-permute-start | bytes 1572872 | tf_op jit(solution)/shard_map/ppermute | solution.py:354
  42.1 2.1 %copy-start.11 = (s32[128]{0:T(128)}, s32[128]{0:T(128)S(1)}, u32[]{:S(2)}) copy-start(s32[128]{0:T(128)S(1)} %get-tuple-element.23.rec_ref) | copy-start | bytes 1540
  42.8 1.4 copy-start.6
  42.8 1.4 copy-start.7
  42.9 1.4 copy-start.8
  43.2 0.9 copy-start.9
  123.7 2.9 %collective-permute-start.10 = (f32[8,256,128]{2,1,0:T(8,128)}, f32[8,256,128]{2,1,0:T(8,128)S(1)}, u32[]{:S(2)}, u32[]{:S(2)}) collective-permute-start(f32[8,256,128]{2,1,0:T(8,128)} %get-tuple-element.8), channel_id=1, source_target_pairs={{0,1},{1,0},{2,3},{3,2},{4,5},{5,4},{6,7},{7,6},{8,9},{9,8},{10,11... | collective-permute-start | bytes 3145736 | tf_op jit(solution)/shard_map/ppermute | solution.py:354
  124.1 4.7 %collective-permute-start.14 = (f32[8,256,128]{2,1,0:T(8,128)}, f32[8,256,128]{2,1,0:T(8,128)S(1)}, u32[]{:S(2)}, u32[]{:S(2)}) collective-permute-start(f32[8,256,128]{2,1,0:T(8,128)} %get-tuple-element.10), channel_id=1, source_target_pairs={{0,1},{1,0},{2,3},{3,2},{4,5},{5,4},{6,7},{7,6},{8,9},{9,8},{10,11... | collective-permute-start | bytes 3145736 | tf_op jit(solution)/shard_map/ppermute | solution.py:354
  126.6 2.2 %copy-start.3 = (f32[8,256,128]{2,1,0:T(8,128)S(1)}, f32[8,256,128]{2,1,0:T(8,128)}, u32[]{:S(2)}) copy-start(f32[8,256,128]{2,1,0:T(8,128)} %get-tuple-element.9) | copy-start | bytes 3145732
  128.2 14.3 %collective-permute-start.11 = (f32[4,256,128]{2,1,0:T(8,128)S(1)}, f32[4,256,128]{2,1,0:T(8,128)S(1)}, u32[]{:S(2)}, u32[]{:S(2)}) collective-permute-start(f32[4,256,128]{2,1,0:T(8,128)S(1)} %slice.59), channel_id=1, source_target_pairs={{0,2},{1,3},{2,0},{3,1},{4,6},{5,7},{6,4},{7,5},{8,10},{9,11},{10,... | collective-permute-start | bytes 1572872 | tf_op jit(solution)/shard_map/ppermute | solution.py:354
  128.9 18.0 %copy-start.10 = (f32[128,16]{1,0:T(8,128)S(1)}, f32[128,16]{1,0:T(8,128)}, u32[]{:S(2)}) copy-start(f32[128,16]{1,0:T(8,128)} %get-tuple-element.11) | copy-start | bytes 24580
  128.9 15.4 %collective-permute-start.15 = (f32[4,256,128]{2,1,0:T(8,128)S(1)}, f32[4,256,128]{2,1,0:T(8,128)S(1)}, u32[]{:S(2)}, u32[]{:S(2)}) collective-permute-start(f32[4,256,128]{2,1,0:T(8,128)S(1)} %slice.65), channel_id=1, source_target_pairs={{0,4},{1,5},{2,6},{3,7},{4,0},{5,1},{6,2},{7,3},{8,12},{9,13},{10,... | collective-permute-start | bytes 1572872 | tf_op jit(solution)/shard_map/ppermute | solution.py:354
  142.5 12.9 %collective-permute-start.12 = (f32[2,256,128]{2,1,0:T(8,128)S(1)}, f32[2,256,128]{2,1,0:T(8,128)S(1)}, u32[]{:S(2)}, u32[]{:S(2)}) collective-permute-start(f32[2,256,128]{2,1,0:T(8,128)S(1)} %slice.61), channel_id=1, source_target_pairs={{0,4},{1,5},{2,6},{3,7},{4,0},{5,1},{6,2},{7,3},{8,12},{9,13},{10,... | collective-permute-start | bytes 786440 | tf_op jit(solution)/shard_map/ppermute | solution.py:354
  144.4 17.4 %collective-permute-start.16 = (f32[2,256,128]{2,1,0:T(8,128)S(1)}, f32[2,256,128]{2,1,0:T(8,128)S(1)}, u32[]{:S(2)}, u32[]{:S(2)}) collective-permute-start(f32[2,256,128]{2,1,0:T(8,128)S(1)} %slice.67), channel_id=1, source_target_pairs={{0,8},{1,9},{2,10},{3,11},{4,12},{5,13},{6,14},{7,15},{8,0},{9,1},... | collective-permute-start | bytes 786440 | tf_op jit(solution)/shard_map/ppermute | solution.py:354
  155.4 8.7 %collective-permute-start.13 = (f32[1,256,128]{2,1,0:T(8,128)S(1)}, f32[1,256,128]{2,1,0:T(8,128)S(1)}, u32[]{:S(2)}, u32[]{:S(2)}) collective-permute-start(f32[1,256,128]{2,1,0:T(8,128)S(1)} %slice.63), channel_id=1, source_target_pairs={{0,8},{1,9},{2,10},{3,11},{4,12},{5,13},{6,14},{7,15},{8,0},{9,1},... | collective-permute-start | bytes 393224 | tf_op jit(solution)/shard_map/ppermute | solution.py:354
  161.8 5.0 %collective-permute-start.17 = (f32[1,256,128]{2,1,0:T(8,128)S(1)}, f32[1,256,128]{2,1,0:T(8,128)S(1)}, u32[]{:S(2)}, u32[]{:S(2)}) collective-permute-start(f32[1,256,128]{2,1,0:T(8,128)S(1)} %slice.69), channel_id=1, source_target_pairs={{0,2},{1,3},{2,0},{3,1},{4,6},{5,7},{6,4},{7,5},{8,10},{9,11},{10,... | collective-permute-start | bytes 393224 | tf_op jit(solution)/shard_map/ppermute | solution.py:354

commit v5 on v4

--- a/solution.py
+++ b/solution.py
@@ -98,7 +98,7 @@
             rec_rows[n, pl.ds(r, 1), :] = fields[to][pl.ds(edge + rec_ref[r], 1), :]
             return 0
 
-        lax.fori_loop(0, nrec, body, 0, unroll=64)
+        lax.fori_loop(0, nrec, body, 0, unroll=True)
 
     def multiply(base, of, taps):
         both = halves[of][pl.ds(base, block), :]
@@ -225,14 +225,14 @@
             moved[pl.ds(r, 1), :] = rate[pl.ds(rec_ref[r], 1), :]
             return 0
 
-        lax.fori_loop(0, nrec, take, 0, unroll=64)
+        lax.fori_loop(0, nrec, take, 0, unroll=True)
         moved[...] = moved[...] + rec_rows[n]
 
         def put(r, _):
             rate[pl.ds(rec_ref[r], 1), :] = moved[pl.ds(r, 1), :]
             return 0
 
-        lax.fori_loop(0, nrec, put, 0, unroll=64)
+        lax.fori_loop(0, nrec, put, 0, unroll=True)
 
     def clear(at):
         rate[pl.ds(at, 16), :] = jnp.zeros((16, LANES), jnp.float32)

time: 168 us -> 165 us (0.982)
  Pallas kernels: 79.4 us -> 76.6 us
    pallas_call x1, Pallas kernels: 79.4 us -> 76.6 us  [shot(): pl.pallas_call(functools.partial(kernel, len(pieces), targets), out_shape...]
where the time goes in v5:
time: 165 us
  Pallas kernels  76.6 us (46%)
  waiting for transfers between devices  52.6 us (32%)
  starting transfers between devices  19.9 us (12%)
  other arithmetic  9.7 us (6%)
  local copies, waits for them, and re-layouts  4.91 us (3%)
    pallas_call x1, Pallas kernels, shot(): pl.pallas_call(functools.partial(kernel, len(pieces), targets), out_shape...  76.6 us
    ppermute x18, waiting for transfers between devices, trade(): lax.ppermute(block, 'shot', [(i, i ^ flip) for i in range(SIDE_Z * SIDE_Y...  52.6 us
    ppermute x18, starting transfers between devices, trade(): lax.ppermute(block, 'shot', [(i, i ^ flip) for i in range(SIDE_Z * SIDE_Y...  19.9 us
    scatter-add x1, other arithmetic, shards(): jnp.zeros((cells * nz,), jnp.float32).at[source_at[0]].add(source_amp[0])  3.55 us
  transfers between devices with their start and end apart: 18, of which 12 were waited for; matrix products, arithmetic and copies ran while one was open for 7% of the time, Pallas kernels for 0%

profile of v5, /device:TPU:0, one launch (start us, length us, event | category | flops | bytes accessed | tf_op | source)
XLA Modules:
  0.0 164.7 jit_solution(14916156780147359732)
XLA Ops:
  0.6 0.0 copy-start
  0.6 1.0 fusion.6
  1.6 3.0 %collective-permute-start.2 = (f32[1,4,64,128]{3,2,1,0:T(8,128)S(1)}, f32[1,4,64,128]{3,2,1,0:T(8,128)S(1)}, u32[]{:S(2)}, u32[]{:S(2)}) collective-permute-start(f32[1,4,64,128]{3,2,1,0:T(8,128)S(1)} %get-tuple-element.20), channel_id=1, source_target_pairs={{0,2},{1,3},{2,0},{3,1},{4,6},{5,7},{6,4},{7,5},{8,10},{9,11},{10,... | collective-permute-start | bytes 393224 | tf_op jit(solution)/shard_map/ppermute | solution.py:354
  4.7 2.6 %collective-permute-start = (f32[1,4,64,128]{3,2,1,0:T(8,128)S(1)}, f32[1,4,64,128]{3,2,1,0:T(8,128)S(1)}, u32[]{:S(2)}, u32[]{:S(2)}) collective-permute-start(f32[1,4,64,128]{3,2,1,0:T(8,128)S(1)} %get-tuple-element.21), channel_id=1, source_target_pairs={{0,8},{1,9},{2,10},{3,11},{4,12},{5,13},{6,14},{7,15},{8,0},{9,1},... | collective-permute-start | bytes 393224 | tf_op jit(solution)/shard_map/ppermute | solution.py:354
  7.3 0.7 compare_select_fusion
  7.9 0.7 fusion.3
  8.6 1.4 copy.20
  10.0 3.3 %collective-permute-done = f32[1,4,64,128]{3,2,1,0:T(8,128)S(1)} collective-permute-done((f32[1,4,64,128]{3,2,1,0:T(8,128)S(1)}, f32[1,4,64,128]{3,2,1,0:T(8,128)S(1)}, u32[]{:S(2)}, u32[]{:S(2)}) %collective-permute-start) | collective-permute-done | bytes 131104 | tf_op jit(solution)/shard_map/ppermute | solution.py:354
  13.4 0.7 collective-permute-start.1
  14.1 0.0 collective-permute-done.2
  14.1 3.4 %collective-permute-start.3 = (f32[2,4,64,128]{3,2,1,0:T(8,128)S(1)}, f32[2,4,64,128]{3,2,1,0:T(8,128)S(1)}, u32[]{:S(2)}, u32[]{:S(2)}) collective-permute-start(f32[2,4,64,128]{3,2,1,0:T(8,128)S(1)} %pad_maximum_fusion.3), channel_id=1, source_target_pairs={{0,8},{1,9},{2,10},{3,11},{4,12},{5,13},{6,14},{7,15},{8,0},{9,1},... | collective-permute-start | bytes 786440 | tf_op jit(solution)/shard_map/ppermute | solution.py:354
  17.6 0.7 fusion.5
  18.2 7.7 %collective-permute-done.1 = f32[2,4,64,128]{3,2,1,0:T(8,128)S(1)} collective-permute-done((f32[2,4,64,128]{3,2,1,0:T(8,128)S(1)}, f32[2,4,64,128]{3,2,1,0:T(8,128)S(1)}, u32[]{:S(2)}, u32[]{:S(2)}) %collective-permute-start.1) | collective-permute-done | bytes 262176 | tf_op jit(solution)/shard_map/ppermute | solution.py:354
  25.9 0.0 copy-start.1
  25.9 0.0 copy-start.16
  26.0 0.0 copy-start.12
  26.0 0.0 copy-start.13
  26.0 0.0 copy-start.14
  26.0 0.0 copy-start.15
  26.0 0.0 copy-start.17
  26.0 0.6 collective-permute-start.4
  26.6 2.8 %collective-permute-done.3 = f32[2,4,64,128]{3,2,1,0:T(8,128)S(1)} collective-permute-done((f32[2,4,64,128]{3,2,1,0:T(8,128)S(1)}, f32[2,4,64,128]{3,2,1,0:T(8,128)S(1)}, u32[]{:S(2)}, u32[]{:S(2)}) %collective-permute-start.3) | collective-permute-done | bytes 262176 | tf_op jit(solution)/shard_map/ppermute | solution.py:354
  29.5 0.3 collective-permute-start.5
  29.8 0.7 gather_fusion
  30.5 3.6 %scatter_custom_fusion = f32[524288]{0:T(1024)} fusion(s32[256]{0:T(256)S(1)} %bitcast.59, f32[256]{0:T(256)} %bitcast.60, f32[]{:T(128)} %constant.68.clone.1), kind=kCustom, calls=%fused_computation.2 | custom fusion | flops 256 | bytes 2097664 | tf_op jit(solution)/shard_map/scatter-add | solution.py:422
  34.1 0.1 collective-permute-start.6
  34.2 0.5 collective-permute-start.7
  34.7 2.8 %collective-permute-done.4 = f32[4,4,64,128]{3,2,1,0:T(8,128)S(1)} collective-permute-done((f32[4,4,64,128]{3,2,1,0:T(8,128)S(1)}, f32[4,4,64,128]{3,2,1,0:T(8,128)S(1)}, u32[]{:S(2)}, u32[]{:S(2)}) %collective-permute-start.4) | collective-permute-done | bytes 524320 | tf_op jit(solution)/shard_map/ppermute | solution.py:354
  37.5 0.0 collective-permute-start.8
  37.5 3.8 %collective-permute-done.5 = f32[4,4,64,128]{3,2,1,0:T(8,128)S(1)} collective-permute-done((f32[4,4,64,128]{3,2,1,0:T(8,128)S(1)}, f32[4,4,64,128]{3,2,1,0:T(8,128)S(1)}, u32[]{:S(2)}, u32[]{:S(2)}) %collective-permute-start.5) | collective-permute-done | bytes 524320 | tf_op jit(solution)/shard_map/ppermute | solution.py:354
  41.3 0.0 collective-permute-start.9
  41.3 0.7 select_reduce_fusion
  42.0 0.0 copy-done.17
  42.1 0.8 fusion.2
  42.8 0.0 collective-permute-done.6
  42.8 0.0 collective-permute-done.7
  42.8 0.0 collective-permute-done.8
  42.9 0.4 collective-permute-done.9
  43.2 0.9 copy-done.9
  44.2 0.0 copy-done.1
  44.2 0.0 copy-done.4
  44.2 76.6 %shot_gradient.1 = (f32[8,256,128]{2,1,0:T(8,128)}, f32[8,256,128]{2,1,0:T(8,128)}, f32[8,256,128]{2,1,0:T(8,128)}, f32[8,256,128]{2,1,0:T(8,128)}, f32[128,16]{1,0:T(8,128)}) custom-call(s32[32]{0:T(128)} %get-tuple-element.19.take_ref, s32[32]{0:T(128)} %get-tuple-element.18.give_ref, s32[128]{0:T(128)} %copy-done.11, f32[16]{0:T(128)} %wav_ref.1, ...), custom_call_target="tpu_custom_call" | custom-call | tf_op jit(solution)/shard_map/shot_gradient/pallas_call | solution.py:307
  120.8 0.5 collective-permute-start.10
  121.3 0.1 collective-permute-start.14
  121.4 2.4 %collective-permute-done.10 = f32[8,256,128]{2,1,0:T(8,128)S(1)} collective-permute-done((f32[8,256,128]{2,1,0:T(8,128)}, f32[8,256,128]{2,1,0:T(8,128)S(1)}, u32[]{:S(2)}, u32[]{:S(2)}) %collective-permute-start.10) | collective-permute-done | bytes 1048608 | tf_op jit(solution)/shard_map/ppermute | solution.py:354
  123.8 1.5 add.84
  125.4 0.5 collective-permute-start.11
  125.9 0.0 collective-permute-done.14
  125.9 0.1 add.88
  126.1 1.8 %collective-permute-start.15 = (f32[4,256,128]{2,1,0:T(8,128)S(1)}, f32[4,256,128]{2,1,0:T(8,128)S(1)}, u32[]{:S(2)}, u32[]{:S(2)}) collective-permute-start(f32[4,256,128]{2,1,0:T(8,128)S(1)} %slice.65), channel_id=1, source_target_pairs={{0,4},{1,5},{2,6},{3,7},{4,0},{5,1},{6,2},{7,3},{8,12},{9,13},{10,... | collective-permute-start | bytes 1572872 | tf_op jit(solution)/shard_map/ppermute | solution.py:354
  127.9 11.7 %collective-permute-done.11 = f32[4,256,128]{2,1,0:T(8,128)S(1)} collective-permute-done((f32[4,256,128]{2,1,0:T(8,128)S(1)}, f32[4,256,128]{2,1,0:T(8,128)S(1)}, u32[]{:S(2)}, u32[]{:S(2)}) %collective-permute-start.11) | collective-permute-done | bytes 524320 | tf_op jit(solution)/shard_map/ppermute | solution.py:354
  139.6 0.1 slice_add_fusion.1
  139.7 1.7 %collective-permute-start.12 = (f32[2,256,128]{2,1,0:T(8,128)S(1)}, f32[2,256,128]{2,1,0:T(8,128)S(1)}, u32[]{:S(2)}, u32[]{:S(2)}) collective-permute-start(f32[2,256,128]{2,1,0:T(8,128)S(1)} %slice.61), channel_id=1, source_target_pairs={{0,4},{1,5},{2,6},{3,7},{4,0},{5,1},{6,2},{7,3},{8,12},{9,13},{10,... | collective-permute-start | bytes 786440 | tf_op jit(solution)/shard_map/ppermute | solution.py:354
  141.4 0.0 collective-permute-done.15
  141.4 0.1 slice_add_fusion
  141.5 2.5 %collective-permute-start.16 = (f32[2,256,128]{2,1,0:T(8,128)S(1)}, f32[2,256,128]{2,1,0:T(8,128)S(1)}, u32[]{:S(2)}, u32[]{:S(2)}) collective-permute-start(f32[2,256,128]{2,1,0:T(8,128)S(1)} %slice.67), channel_id=1, source_target_pairs={{0,8},{1,9},{2,10},{3,11},{4,12},{5,13},{6,14},{7,15},{8,0},{9,1},... | collective-permute-start | bytes 786440 | tf_op jit(solution)/shard_map/ppermute | solution.py:354
  144.0 0.7 copy.21
  144.7 8.0 %collective-permute-done.12 = f32[2,256,128]{2,1,0:T(8,128)S(1)} collective-permute-done((f32[2,256,128]{2,1,0:T(8,128)S(1)}, f32[2,256,128]{2,1,0:T(8,128)S(1)}, u32[]{:S(2)}, u32[]{:S(2)}) %collective-permute-start.12) | collective-permute-done | bytes 262176 | tf_op jit(solution)/shard_map/ppermute | solution.py:354
  152.7 1.0 collective-permute-start.13
  153.7 5.1 %collective-permute-done.16 = f32[2,256,128]{2,1,0:T(8,128)S(1)} collective-permute-done((f32[2,256,128]{2,1,0:T(8,128)S(1)}, f32[2,256,128]{2,1,0:T(8,128)S(1)}, u32[]{:S(2)}, u32[]{:S(2)}) %collective-permute-start.16) | collective-permute-done | bytes 262176 | tf_op jit(solution)/shard_map/ppermute | solution.py:354
  158.9 0.5 collective-permute-start.17
  159.4 1.8 %collective-permute-done.13 = f32[1,256,128]{2,1,0:T(8,128)S(1)} collective-permute-done((f32[1,256,128]{2,1,0:T(8,128)S(1)}, f32[1,256,128]{2,1,0:T(8,128)S(1)}, u32[]{:S(2)}, u32[]{:S(2)}) %collective-permute-start.13) | collective-permute-done | bytes 131104 | tf_op jit(solution)/shard_map/ppermute | solution.py:354
  161.2 2.7 %collective-permute-done.17 = f32[1,256,128]{2,1,0:T(8,128)S(1)} collective-permute-done((f32[1,256,128]{2,1,0:T(8,128)S(1)}, f32[1,256,128]{2,1,0:T(8,128)S(1)}, u32[]{:S(2)}, u32[]{:S(2)}) %collective-permute-start.17) | collective-permute-done | bytes 131104 | tf_op jit(solution)/shard_map/ppermute | solution.py:354
  163.9 0.7 pad_maximum_fusion.4
  (42 shorter events, 0.4 us)
Async XLA Ops:
  0.6 29.2 %copy-start = (s32[32]{0:T(128)S(1)}, s32[32]{0:T(128)}, u32[]{:S(2)}) copy-start(s32[32]{0:T(128)} %param.15) | copy-start | bytes 388
  1.6 12.5 %collective-permute-start.2 = (f32[1,4,64,128]{3,2,1,0:T(8,128)S(1)}, f32[1,4,64,128]{3,2,1,0:T(8,128)S(1)}, u32[]{:S(2)}, u32[]{:S(2)}) collective-permute-start(f32[1,4,64,128]{3,2,1,0:T(8,128)S(1)} %get-tuple-element.20), channel_id=1, source_target_pairs={{0,2},{1,3},{2,0},{3,1},{4,6},{5,7},{6,4},{7,5},{8,10},{9,11},{10,... | collective-permute-start | bytes 393224 | tf_op jit(solution)/shard_map/ppermute | solution.py:354
  4.7 8.7 %collective-permute-start = (f32[1,4,64,128]{3,2,1,0:T(8,128)S(1)}, f32[1,4,64,128]{3,2,1,0:T(8,128)S(1)}, u32[]{:S(2)}, u32[]{:S(2)}) collective-permute-start(f32[1,4,64,128]{3,2,1,0:T(8,128)S(1)} %get-tuple-element.21), channel_id=1, source_target_pairs={{0,8},{1,9},{2,10},{3,11},{4,12},{5,13},{6,14},{7,15},{8,0},{9,1},... | collective-permute-start | bytes 393224 | tf_op jit(solution)/shard_map/ppermute | solution.py:354
  13.4 12.5 %collective-permute-start.1 = (f32[2,4,64,128]{3,2,1,0:T(8,128)S(1)}, f32[2,4,64,128]{3,2,1,0:T(8,128)S(1)}, u32[]{:S(2)}, u32[]{:S(2)}) collective-permute-start(f32[2,4,64,128]{3,2,1,0:T(8,128)S(1)} %pad_maximum_fusion.2), channel_id=1, source_target_pairs={{0,4},{1,5},{2,6},{3,7},{4,0},{5,1},{6,2},{7,3},{8,12},{9,13},{10,... | collective-permute-start | bytes 786440 | tf_op jit(solution)/shard_map/ppermute | solution.py:354
  14.1 15.3 %collective-permute-start.3 = (f32[2,4,64,128]{3,2,1,0:T(8,128)S(1)}, f32[2,4,64,128]{3,2,1,0:T(8,128)S(1)}, u32[]{:S(2)}, u32[]{:S(2)}) collective-permute-start(f32[2,4,64,128]{3,2,1,0:T(8,128)S(1)} %pad_maximum_fusion.3), channel_id=1, source_target_pairs={{0,8},{1,9},{2,10},{3,11},{4,12},{5,13},{6,14},{7,15},{8,0},{9,1},... | collective-permute-start | bytes 786440 | tf_op jit(solution)/shard_map/ppermute | solution.py:354
  25.9 18.3 %copy-start.1 = (f32[4,4,64,128]{3,2,1,0:T(8,128)}, f32[4,4,64,128]{3,2,1,0:T(8,128)S(1)}, u32[]{:S(2)}) copy-start(f32[4,4,64,128]{3,2,1,0:T(8,128)S(1)} %pad_maximum_fusion) | copy-start | bytes 1572868
  25.9 8.1 %copy-start.16 = (s32[1,16]{1,0:T(1,128)S(1)}, s32[1,16]{1,0:T(1,128)}, u32[]{:S(2)}) copy-start(s32[1,16]{1,0:T(1,128)} %param.16) | copy-start | bytes 196
  26.0 8.1 %copy-start.12 = (s32[32]{0:T(128)S(1)}, s32[32]{0:T(128)}, u32[]{:S(2)}) copy-start(s32[32]{0:T(128)} %constant.74.clone) | copy-start | bytes 388
  26.0 8.1 %copy-start.13 = (s32[32]{0:T(128)S(1)}, s32[32]{0:T(128)}, u32[]{:S(2)}) copy-start(s32[32]{0:T(128)} %constant.73.clone) | copy-start | bytes 388
  26.0 8.1 %copy-start.14 = (s32[32]{0:T(128)S(1)}, s32[32]{0:T(128)}, u32[]{:S(2)}) copy-start(s32[32]{0:T(128)} %constant.72.clone) | copy-start | bytes 388
  26.0 8.1 %copy-start.15 = (s32[32]{0:T(128)S(1)}, s32[32]{0:T(128)}, u32[]{:S(2)}) copy-start(s32[32]{0:T(128)} %constant.71.clone) | copy-start | bytes 388
  26.0 16.0 %copy-start.17 = (s32[1,128]{1,0:T(1,128)S(1)}, s32[1,128]{1,0:T(1,128)}, u32[]{:S(2)}) copy-start(s32[1,128]{1,0:T(1,128)} %param.19) | copy-start | bytes 1540
  26.0 11.5 %collective-permute-start.4 = (f32[4,4,64,128]{3,2,1,0:T(8,128)S(1)}, f32[4,4,64,128]{3,2,1,0:T(8,128)S(1)}, u32[]{:S(2)}, u32[]{:S(2)}) collective-permute-start(f32[4,4,64,128]{3,2,1,0:T(8,128)S(1)} %pad_maximum_fusion), channel_id=1, source_target_pairs={{0,2},{1,3},{2,0},{3,1},{4,6},{5,7},{6,4},{7,5},{8,10},{9,11},{10,... | collective-permute-start | bytes 1572872 | tf_op jit(solution)/shard_map/ppermute | solution.py:354
  29.5 14.7 %copy-start.2 = (f32[4,4,64,128]{3,2,1,0:T(8,128)}, f32[4,4,64,128]{3,2,1,0:T(8,128)S(1)}, u32[]{:S(2)}) copy-start(f32[4,4,64,128]{3,2,1,0:T(8,128)S(1)} %pad_maximum_fusion.1) | copy-start | bytes 1572868
  29.5 11.8 %collective-permute-start.5 = (f32[4,4,64,128]{3,2,1,0:T(8,128)S(1)}, f32[4,4,64,128]{3,2,1,0:T(8,128)S(1)}, u32[]{:S(2)}, u32[]{:S(2)}) collective-permute-start(f32[4,4,64,128]{3,2,1,0:T(8,128)S(1)} %pad_maximum_fusion.1), channel_id=1, source_target_pairs={{0,4},{1,5},{2,6},{3,7},{4,0},{5,1},{6,2},{7,3},{8,12},{9,13},{10,... | collective-permute-start | bytes 1572872 | tf_op jit(solution)/shard_map/ppermute | solution.py:354
  34.1 8.7 %collective-permute-start.6 = (f32[4,4,64,128]{3,2,1,0:T(8,128)S(1)}, f32[4,4,64,128]{3,2,1,0:T(8,128)S(1)}, u32[]{:S(2)}, u32[]{:S(2)}) collective-permute-start(f32[4,4,64,128]{3,2,1,0:T(8,128)S(1)} %pad_maximum_fusion), channel_id=1, source_target_pairs={{0,1},{1,0},{2,3},{3,2},{4,5},{5,4},{6,7},{7,6},{8,9},{9,8},{10,11... | collective-permute-start | bytes 1572872 | tf_op jit(solution)/shard_map/ppermute | solution.py:354
  34.2 8.7 %collective-permute-start.7 = (f32[4,4,64,128]{3,2,1,0:T(8,128)S(1)}, f32[4,4,64,128]{3,2,1,0:T(8,128)S(1)}, u32[]{:S(2)}, u32[]{:S(2)}) collective-permute-start(f32[4,4,64,128]{3,2,1,0:T(8,128)S(1)} %pad_maximum_fusion.1), channel_id=1, source_target_pairs={{0,1},{1,0},{2,3},{3,2},{4,5},{5,4},{6,7},{7,6},{8,9},{9,8},{10,11... | collective-permute-start | bytes 1572872 | tf_op jit(solution)/shard_map/ppermute | solution.py:354
  37.5 6.7 %copy-start.4 = (f32[4,4,64,128]{3,2,1,0:T(8,128)}, f32[4,4,64,128]{3,2,1,0:T(8,128)S(1)}, u32[]{:S(2)}) copy-start(f32[4,4,64,128]{3,2,1,0:T(8,128)S(1)} %collective-permute-done.4) | copy-start | bytes 1572868
  37.5 5.3 %collective-permute-start.8 = (f32[4,4,64,128]{3,2,1,0:T(8,128)S(1)}, f32[4,4,64,128]{3,2,1,0:T(8,128)S(1)}, u32[]{:S(2)}, u32[]{:S(2)}) collective-permute-start(f32[4,4,64,128]{3,2,1,0:T(8,128)S(1)} %collective-permute-done.4), channel_id=1, source_target_pairs={{0,1},{1,0},{2,3},{3,2},{4,5},{5,4},{6,7},{7,6},{8,9},{9,8},{10,11... | collective-permute-start | bytes 1572872 | tf_op jit(solution)/shard_map/ppermute | solution.py:354
  41.3 2.9 %copy-start.5 = (f32[4,4,64,128]{3,2,1,0:T(8,128)}, f32[4,4,64,128]{3,2,1,0:T(8,128)S(1)}, u32[]{:S(2)}) copy-start(f32[4,4,64,128]{3,2,1,0:T(8,128)S(1)} %collective-permute-done.5) | copy-start | bytes 1572868
  41.3 1.9 %collective-permute-start.9 = (f32[4,4,64,128]{3,2,1,0:T(8,128)S(1)}, f32[4,4,64,128]{3,2,1,0:T(8,128)S(1)}, u32[]{:S(2)}, u32[]{:S(2)}) collective-permute-start(f32[4,4,64,128]{3,2,1,0:T(8,128)S(1)} %collective-permute-done.5), channel_id=1, source_target_pairs={{0,1},{1,0},{2,3},{3,2},{4,5},{5,4},{6,7},{7,6},{8,9},{9,8},{10,11... | collective-permute-start | bytes 1572872 | tf_op jit(solution)/shard_map/ppermute | solution.py:354
  42.1 2.1 %copy-start.11 = (s32[128]{0:T(128)}, s32[128]{0:T(128)S(1)}, u32[]{:S(2)}) copy-start(s32[128]{0:T(128)S(1)} %get-tuple-element.23.rec_ref) | copy-start | bytes 1540
  42.8 1.4 copy-start.6
  42.8 1.4 copy-start.7
  42.9 1.4 copy-start.8
  43.2 0.9 copy-start.9
  120.8 3.0 %collective-permute-start.10 = (f32[8,256,128]{2,1,0:T(8,128)}, f32[8,256,128]{2,1,0:T(8,128)S(1)}, u32[]{:S(2)}, u32[]{:S(2)}) collective-permute-start(f32[8,256,128]{2,1,0:T(8,128)} %get-tuple-element.8), channel_id=1, source_target_pairs={{0,1},{1,0},{2,3},{3,2},{4,5},{5,4},{6,7},{7,6},{8,9},{9,8},{10,11... | collective-permute-start | bytes 3145736 | tf_op jit(solution)/shard_map/ppermute | solution.py:354
  121.3 4.6 %collective-permute-start.14 = (f32[8,256,128]{2,1,0:T(8,128)}, f32[8,256,128]{2,1,0:T(8,128)S(1)}, u32[]{:S(2)}, u32[]{:S(2)}) collective-permute-start(f32[8,256,128]{2,1,0:T(8,128)} %get-tuple-element.10), channel_id=1, source_target_pairs={{0,1},{1,0},{2,3},{3,2},{4,5},{5,4},{6,7},{7,6},{8,9},{9,8},{10,11... | collective-permute-start | bytes 3145736 | tf_op jit(solution)/shard_map/ppermute | solution.py:354
  123.8 2.1 %copy-start.3 = (f32[8,256,128]{2,1,0:T(8,128)S(1)}, f32[8,256,128]{2,1,0:T(8,128)}, u32[]{:S(2)}) copy-start(f32[8,256,128]{2,1,0:T(8,128)} %get-tuple-element.9) | copy-start | bytes 3145732
  125.4 14.3 %collective-permute-start.11 = (f32[4,256,128]{2,1,0:T(8,128)S(1)}, f32[4,256,128]{2,1,0:T(8,128)S(1)}, u32[]{:S(2)}, u32[]{:S(2)}) collective-permute-start(f32[4,256,128]{2,1,0:T(8,128)S(1)} %slice.59), channel_id=1, source_target_pairs={{0,2},{1,3},{2,0},{3,1},{4,6},{5,7},{6,4},{7,5},{8,10},{9,11},{10,... | collective-permute-start | bytes 1572872 | tf_op jit(solution)/shard_map/ppermute | solution.py:354
  126.0 18.0 %copy-start.10 = (f32[128,16]{1,0:T(8,128)S(1)}, f32[128,16]{1,0:T(8,128)}, u32[]{:S(2)}) copy-start(f32[128,16]{1,0:T(8,128)} %get-tuple-element.11) | copy-start | bytes 24580
  126.1 15.4 %collective-permute-start.15 = (f32[4,256,128]{2,1,0:T(8,128)S(1)}, f32[4,256,128]{2,1,0:T(8,128)S(1)}, u32[]{:S(2)}, u32[]{:S(2)}) collective-permute-start(f32[4,256,128]{2,1,0:T(8,128)S(1)} %slice.65), channel_id=1, source_target_pairs={{0,4},{1,5},{2,6},{3,7},{4,0},{5,1},{6,2},{7,3},{8,12},{9,13},{10,... | collective-permute-start | bytes 1572872 | tf_op jit(solution)/shard_map/ppermute | solution.py:354
  139.7 13.0 %collective-permute-start.12 = (f32[2,256,128]{2,1,0:T(8,128)S(1)}, f32[2,256,128]{2,1,0:T(8,128)S(1)}, u32[]{:S(2)}, u32[]{:S(2)}) collective-permute-start(f32[2,256,128]{2,1,0:T(8,128)S(1)} %slice.61), channel_id=1, source_target_pairs={{0,4},{1,5},{2,6},{3,7},{4,0},{5,1},{6,2},{7,3},{8,12},{9,13},{10,... | collective-permute-start | bytes 786440 | tf_op jit(solution)/shard_map/ppermute | solution.py:354
  141.5 17.3 %collective-permute-start.16 = (f32[2,256,128]{2,1,0:T(8,128)S(1)}, f32[2,256,128]{2,1,0:T(8,128)S(1)}, u32[]{:S(2)}, u32[]{:S(2)}) collective-permute-start(f32[2,256,128]{2,1,0:T(8,128)S(1)} %slice.67), channel_id=1, source_target_pairs={{0,8},{1,9},{2,10},{3,11},{4,12},{5,13},{6,14},{7,15},{8,0},{9,1},... | collective-permute-start | bytes 786440 | tf_op jit(solution)/shard_map/ppermute | solution.py:354
  152.7 8.5 %collective-permute-start.13 = (f32[1,256,128]{2,1,0:T(8,128)S(1)}, f32[1,256,128]{2,1,0:T(8,128)S(1)}, u32[]{:S(2)}, u32[]{:S(2)}) collective-permute-start(f32[1,256,128]{2,1,0:T(8,128)S(1)} %slice.63), channel_id=1, source_target_pairs={{0,8},{1,9},{2,10},{3,11},{4,12},{5,13},{6,14},{7,15},{8,0},{9,1},... | collective-permute-start | bytes 393224 | tf_op jit(solution)/shard_map/ppermute | solution.py:354
  158.9 5.0 %collective-permute-start.17 = (f32[1,256,128]{2,1,0:T(8,128)S(1)}, f32[1,256,128]{2,1,0:T(8,128)S(1)}, u32[]{:S(2)}, u32[]{:S(2)}) collective-permute-start(f32[1,256,128]{2,1,0:T(8,128)S(1)} %slice.69), channel_id=1, source_target_pairs={{0,2},{1,3},{2,0},{3,1},{4,6},{5,7},{6,4},{7,5},{8,10},{9,11},{10,... | collective-permute-start | bytes 393224 | tf_op jit(solution)/shard_map/ppermute | solution.py:354
